TPU v7x, 512 devices: a whole 4x8x8 slice. The times are simulated.
512 devices in a mesh: replica: 16 (over z, core), table: 32 (over x, y).
Axes of the slice: x: 4, y: 8, z: 8, core: 2. Of those that a mesh axis runs over, the one named last changes fastest.
Arguments:
- table: float32 [32768, 128], P('table'), may hold values from -0.6 to 0.6
- row_state: float32 [32768], P('table'), may hold values from 1.1920929e-08 to 2.3841858e-07
- lookup_grads: bfloat16 [16, 32768, 128], P('replica', 'table'), may hold values from -6 to 6
- lookup_slots: int32 [16, 32768], P('replica', 'table'), may hold values from 0 to 3
- lookup_rows: int32 [16, 32768], P('replica', 'table'), may hold values from 0 to 127
- block_ids: int32 [16, 128], P('replica', 'table'), may hold values from 0 to 7, as said below
- block_counts: int32 [16, 32], P('replica', 'table'), may hold values from 1 to 4, as said below
- inputs: bfloat16 [524288, 512], P(('replica', 'table')), may hold values from -2036.4675 to 2036.4675
- cotangent: bfloat16 [524288, 512], P(('replica', 'table')), may hold values from -45 to 45
- w_first: bfloat16 [512, 512], replicated, may hold values from -0.25 to 0.25
- w_second: bfloat16 [512, 512], replicated, may hold values from -0.25 to 0.25
Outputs:
- new_table: float32 [32768, 128], P('table')
- new_state: float32 [32768], P('table')
- new_first: bfloat16 [512, 512], replicated
- new_second: bfloat16 [512, 512], replicated
Inputs may be any that keep to these rules, and one draw needn't show every extreme that they name: `block_ids`: within one device's 4 entries the block ids are distinct; entries of slots that are not live are not used. `block_counts`: some device uses all 4 slots in every draw.
All inputs are finite; a program needn't handle non-finite values.
Results may differ from a plain program's by a relative error of at most 0.00065.
The roundings to bfloat16 on the way count: a program that leaves them out, or rounds other values in their place, can miss the bound.
Values may be sent and summed in bfloat16 or wider, within the bound.
A program may use at most 64 MiB of HBM per device.

v0:
```python
import jax
import jax.numpy as jnp
from jax import lax
from jax.sharding import PartitionSpec as P

BLOCK_ROWS = 128


emb_rate = 0.05
mlp_rate_unit = 0.04


def slot_blocks(lookup_grads, lookup_slots, lookup_rows, live_count, slot_count, block_rows):
    grad_rows = lookup_grads[0]
    slot_ids = lookup_slots[0]
    position = slot_ids * block_rows + lookup_rows[0]
    targets = jnp.arange(slot_count * block_rows, dtype=jnp.int32)
    onehot = ((position[:, None] == targets[None, :]) & (slot_ids < live_count)[:, None]).astype(
        jnp.bfloat16
    )
    summed = jnp.einsum("lp,le->pe", onehot, grad_rows, preferred_element_type=jnp.float32)
    return summed.astype(jnp.bfloat16).reshape(slot_count, block_rows * grad_rows.shape[1])


def place_blocks(slot_block, slot_live, blocks_flat, block_total):
    targets = jnp.arange(block_total, dtype=jnp.int32)
    select = ((targets[:, None] == slot_block[None, :]) & slot_live[None, :]).astype(jnp.bfloat16)
    return jnp.dot(select, blocks_flat, preferred_element_type=jnp.float32)


def adagrad_rows(table_rows, state_rows, grad_rows, clip_scale):
    clipped = clip_scale * grad_rows
    fresh_state = state_rows + jnp.mean(clipped * clipped, axis=1)
    fresh_table = table_rows - emb_rate * clipped / jnp.sqrt(fresh_state)[:, None]
    return (fresh_table, fresh_state)


def on_device(
    table,
    row_state,
    lookup_grads,
    lookup_slots,
    lookup_rows,
    block_ids,
    block_counts,
    inputs,
    cotangent,
    w_first,
    w_second,
):
    emb_width = table.shape[1]
    block_rows = BLOCK_ROWS
    block_total = table.shape[0] // block_rows
    slot_count = block_ids.shape[1]
    live_count = block_counts[0, 0]
    blocks_flat = slot_blocks(
        lookup_grads, lookup_slots, lookup_rows, live_count, slot_count, block_rows
    )
    slot_live = jnp.arange(slot_count, dtype=jnp.int32) < live_count
    first_replica = lax.axis_index("replica") == 0
    dense_grad = place_blocks(block_ids[0], slot_live, blocks_flat, block_total)
    merged = lax.psum(dense_grad, "replica").reshape(-1, emb_width)
    emb_part = jnp.where(first_replica, jnp.sum(merged * merged), 0.0)
    pre_act = jnp.dot(inputs, w_first, preferred_element_type=jnp.float32)
    sigmoid_pre = jax.nn.sigmoid(pre_act)
    hidden = (pre_act * sigmoid_pre).astype(jnp.bfloat16)
    back_grad = jnp.einsum("bj,ij->bi", cotangent, w_second, preferred_element_type=jnp.float32)
    d_pre = (back_grad * sigmoid_pre * (1.0 + pre_act * (1.0 - sigmoid_pre))).astype(jnp.bfloat16)
    hid_width = w_first.shape[0]
    rate = mlp_rate_unit * hid_width
    grad_first = jnp.einsum("bi,bj->ij", inputs, d_pre, preferred_element_type=jnp.float32)
    grad_second = jnp.einsum("bi,bj->ij", hidden, cotangent, preferred_element_type=jnp.float32)
    grad_first, grad_second = lax.psum((grad_first, grad_second), ("replica", "table"))
    mlp_part = jnp.where(
        first_replica & (lax.axis_index("table") == 0),
        jnp.sum(grad_first * grad_first) + jnp.sum(grad_second * grad_second),
        0.0,
    )
    emb_total, mlp_total = lax.psum((emb_part, mlp_part), ("replica", "table"))
    norm_total = emb_total + mlp_total
    clip_scale = jnp.minimum(1.0, 1.0 / (jnp.sqrt(norm_total) + 1e-06))
    new_table, new_state = adagrad_rows(table, row_state, merged, clip_scale)
    new_first = (w_first.astype(jnp.float32) - rate * clip_scale * grad_first).astype(jnp.bfloat16)
    new_second = (w_second.astype(jnp.float32) - rate * clip_scale * grad_second).astype(
        jnp.bfloat16
    )
    return (new_table, new_state, new_first, new_second)


def solution(mesh):
    placed = (
        P("table", None),
        P("table"),
        P("replica", "table", None),
        P("replica", "table"),
        P("replica", "table"),
        P("replica", "table"),
        P("replica", "table"),
        P(("replica", "table"), None),
        P(("replica", "table"), None),
        P(),
        P(),
    )
    return jax.shard_map(
        on_device,
        mesh=mesh,
        in_specs=placed,
        out_specs=(P("table", None), P("table"), P(), P()),
        check_vma=False,
    )
```

profile of v0, /device:TPU:1, one launch (start us, length us, event | category | flops | bytes accessed | tf_op | source)
XLA Modules:
  0.0 546.2 jit_solution(5682067070631737674)
XLA Ops:
  7.2 0.0 copy-start
  7.2 0.0 all-reduce.4.cloned.1.call-start
  8.0 0.7 compare_reduce_fusion
  8.7 0.7 multiply_add_fusion.1
  9.4 2.0 fusion.3
  11.4 1.7 fusion.12
  13.1 0.0 all-reduce.4.cloned.1.call-update
  13.1 0.0 all-reduce.6.cloned.1.call-start
  13.2 1.7 fusion.19
  14.9 4.0 convolution_bitcast_fusion
  18.9 3.1 fusion.9
  22.0 0.0 all-reduce.6.cloned.1.call-update
  22.1 0.0 copy-start.6
  22.1 1.0 copy-done.3
  23.1 1.0 copy.16
  24.1 110.5 %all-reduce.4.cloned.1.call-done = f32[8,16384]{1,0:T(8,128)} async-done(((f32[8,16384]{1,0:T(8,128)}), f32[8,16384]{1,0:T(8,128)}) %all-reduce.4.cloned.1.call-update) | async-done | bytes 524304 | tf_op jit(solution)/shard_map/psum | solution.py:62
  134.6 1.8 multiply_reduce_fusion.2
  137.0 283.0 %all-reduce.6.cloned.1.call-done = (f32[512,512]{0,1:T(8,128)}, f32[512,512]{0,1:T(8,128)}) async-done(((f32[512,512]{0,1:T(8,128)}, f32[512,512]{0,1:T(8,128)}), (f32[512,512]{0,1:T(8,128)}, f32[512,512]{0,1:T(8,128)})) %all-reduce.6.cloned.1.call-update) | async-done | bytes 2097168 | tf_op jit(solution)/shard_map/psum | solution.py:73
  420.0 2.1 multiply_reduce_fusion
  422.1 2.1 multiply_reduce_fusion.1
  425.6 1.0 copy.17
  426.6 96.4 %psum.40 = f32[]{:T(128)} all-reduce(f32[]{:T(128)S(6)} %add.43), channel_id=1, replica_groups=mesh['replica'=16,'table'=32] {'replica','table'}, use_global_device_ids=true, to_apply=%region_2.3 | all-reduce | flops 1 | bytes 8 | tf_op jit(solution)/shard_map/psum | solution.py:79
  523.7 2.2 multiply_multiply_fusion
  525.9 1.9 mul.84
  527.9 1.2 reduce_sum.39
  529.1 1.9 mul.82
  531.0 0.0 copy-done.2
  531.0 2.5 subtract_convert_fusion
  533.6 2.1 copy.18
  535.7 2.0 copy.19
  537.7 0.6 fusion.18
  538.3 1.0 divide_subtract_fusion
  (14 shorter events, 0.1 us)
Async XLA Ops:
  7.2 6.0 %copy-start = (bf16[1024,512]{1,0:T(8,128)(2,1)S(1)}, bf16[1024,512]{1,0:T(8,128)(2,1)}, u32[]{:S(2)}) copy-start(bf16[1024,512]{1,0:T(8,128)(2,1)} %param.18) | copy-start | bytes 3145732
  7.2 127.4 %all-reduce.4.cloned.1.call-start = ((), (), s32[]{:S(2)}) async-start(), calls=%async_computation | async-start | bytes 1048576 | tf_op jit(solution)/shard_map/psum | solution.py:62
  13.1 406.9 %all-reduce.6.cloned.1.call-start = ((), (), s32[]{:S(2)}) async-start(), calls=%async_computation.1 | async-start | bytes 4194304 | tf_op jit(solution)/shard_map/psum | solution.py:73
  22.0 1.0 copy-start.3
  22.1 403.5 %copy-start.6 = (bf16[512,512]{1,0:T(8,128)(2,1)S(1)}, bf16[512,512]{1,0:T(8,128)(2,1)}, u32[]{:S(2)}) copy-start(bf16[512,512]{1,0:T(8,128)(2,1)} %param.21) | copy-start | bytes 1572868
  523.7 7.3 %copy-start.1 = (f32[512,512]{0,1:T(8,128)S(1)}, f32[512,512]{0,1:T(8,128)}, u32[]{:S(2)}) copy-start(f32[512,512]{0,1:T(8,128)} %get-tuple-element.8) | copy-start | bytes 3145732
  523.7 7.3 %copy-start.2 = (f32[512,512]{0,1:T(8,128)S(1)}, f32[512,512]{0,1:T(8,128)}, u32[]{:S(2)}) copy-start(f32[512,512]{0,1:T(8,128)} %get-tuple-element.9) | copy-start | bytes 3145732
  533.6 4.2 copy-start.7
  533.6 4.8 copy-start.4
  533.6 4.8 copy-start.5
Sparse Core Ops, SparseCore 0:
  13.2 121.3 all-reduce.3
  140.5 279.5 all-reduce.5
where the time goes:
time: 547 us; the launch traced here: 546 us
  waiting for transfers between devices  394 us (72%)
  blocking collectives  96.4 us (18%)
  between operations  17.6 us (3%)
  other arithmetic  15 us (3%)
  matrix products  12.5 us (2%)
  local copies, waits for them, and re-layouts  11.1 us (2%)
    psum x1, waiting for transfers between devices, on_device(): lax.psum((grad_first, grad_second), ('replica', 'table'))  283 us
    psum x1, waiting for transfers between devices, on_device(): merged = lax.psum(dense_grad, 'replica').reshape(-1, emb_width)  110 us
    psum x1, blocking collectives, on_device(): emb_total, mlp_total = lax.psum((emb_part, mlp_part), ('replica', 'table'))  96.4 us
  transfers between devices with their start and end apart: 2, of which 2 were waited for; matrix products, arithmetic and copies ran while one was open for 2% of the time, Pallas kernels for 0%

commit v1 on v0

v1 whole, which is shorter than its diff:
```python
import jax
import jax.numpy as jnp
from jax import lax
from jax.experimental import pallas as pl
from jax.experimental.pallas import tpu as pltpu
from jax.sharding import PartitionSpec as P

X, Y, Z, C = 4, 8, 8, 2
BLOCK_ROWS = 128
EMB = 128
HID = 512
SLOTS = 4
BLOCKS = 8
SAMPLES = 1024
LOOKUPS = 1024
ROWS = BLOCKS * BLOCK_ROWS
SHARE = ROWS // (Z * C)
CHUNK = 256

EMB_RATE = 0.05
MLP_RATE = 0.04 * HID
F32 = jnp.float32
BF16 = jnp.bfloat16
MESH = pl.DeviceIdType.MESH


def kernel(
    table_hbm, state_ref, grads_hbm, slots_ref, rows_ref, ids_ref, count_ref,
    inputs_hbm, cot_hbm, w1_hbm, w2_hbm,
    new_table, new_state, new_first, new_second,
    table, lgrads, w1, w2, left, right,
    dense, emb_recv, merged,
    g_sib, g_own, g_recv,
    r1x, r1y, r1z, t2y, t2z, r2y, r2z, r3x, r3y, r3z, w4y, w4z, f5x, f5y, f5z,
    in_sem, send_sem, recv_sem,
):
    rep = lax.axis_index("replica")
    tab = lax.axis_index("table")
    z, c = rep // C, lax.rem(rep, C)
    x, y = tab // Y, lax.rem(tab, Y)
    sib = 1 - c

    def at_x(d):
        return (rep, lax.rem(x + d, X) * Y + y)

    def at_y(d):
        return (rep, x * Y + lax.rem(y + d, Y))

    def at_z(d, core=c):
        return (lax.rem(z + d, Z) * C + core, tab)

    sibling = (z * C + sib, tab)

    def send(src, dst, k, dev):
        pltpu.make_async_remote_copy(
            src_ref=src, dst_ref=dst, send_sem=send_sem.at[k], recv_sem=recv_sem.at[k],
            device_id=dev, device_id_type=MESH,
        ).start()

    def take(ref, k):
        pltpu.make_async_copy(ref, ref, recv_sem.at[k]).wait()

    def sent(ref, k):
        pltpu.make_async_copy(ref, ref, send_sem.at[k]).wait()

    loads = [
        pltpu.make_async_copy(grads_hbm.at[0], lgrads, in_sem.at[0]),
        pltpu.make_async_copy(w1_hbm, w1, in_sem.at[1]),
        pltpu.make_async_copy(inputs_hbm, left.at[0], in_sem.at[2]),
        pltpu.make_async_copy(w2_hbm, w2, in_sem.at[3]),
        pltpu.make_async_copy(cot_hbm, right.at[1], in_sem.at[4]),
        pltpu.make_async_copy(table_hbm, table, in_sem.at[5]),
    ]
    for load in loads:
        load.start()

    barrier = pltpu.get_barrier_semaphore()
    peers = [at_x(d) for d in range(1, X)] + [at_y(d) for d in range(1, Y)]
    peers += [at_z(d) for d in range(1, Z)] + [at_z(d, sib) for d in range(Z)]
    for dev in peers:
        pl.semaphore_signal(barrier, inc=1, device_id=dev, device_id_type=MESH)

    count = count_ref[0, 0]
    slot_ids = slots_ref[...]
    position = jnp.where(slot_ids < count, slot_ids * BLOCK_ROWS + rows_ref[...], -1)
    loads[0].wait()
    lookup_grads = lgrads[...]
    slot_sums = []
    for k in range(SLOTS):
        target = lax.broadcasted_iota(jnp.int32, (BLOCK_ROWS, LOOKUPS), 0) + k * BLOCK_ROWS
        onehot = jnp.where(target == position, 1.0, 0.0).astype(BF16)
        summed = jnp.dot(onehot, lookup_grads, preferred_element_type=F32)
        slot_sums.append(summed.astype(BF16).astype(F32))
    for b in range(BLOCKS):
        block = jnp.zeros((BLOCK_ROWS, EMB), F32)
        for k in range(SLOTS):
            block += jnp.where((ids_ref[0, k] == b) & (k < count), 1.0, 0.0) * slot_sums[k]
        dense[pl.ds(b * BLOCK_ROWS, BLOCK_ROWS)] = block.astype(BF16)

    def share(zz, cc):
        return pl.ds(pl.multiple_of((cc * Z + zz) * SHARE, SHARE), SHARE)

    pl.semaphore_wait(barrier, len(peers))
    for d in range(Z):
        for same in (True, False):
            if d == 0 and same:
                continue
            core = c if same else sib
            send(dense.at[share(lax.rem(z + d, Z), core)], emb_recv.at[rep], 0, at_z(d, core))
    emb_recv[rep] = dense[share(z, c)]

    for load in loads[1:5]:
        load.wait()

    def mlp(i, _):
        rows = pl.ds(pl.multiple_of(i * CHUNK, CHUNK), CHUNK)
        pre = jnp.dot(left[0, rows], w1[...], preferred_element_type=F32)
        sig = jax.nn.sigmoid(pre)
        left[1, rows] = (pre * sig).astype(BF16)
        back = lax.dot_general(
            right[1, rows], w2[...], (((1,), (1,)), ((), ())), preferred_element_type=F32
        )
        right[0, rows] = (back * sig * (1.0 + pre * (1.0 - sig))).astype(BF16)
        return 0

    lax.fori_loop(0, SAMPLES // CHUNK, mlp, 0)

    def grad(which, half):
        cols = pl.ds(pl.multiple_of(half * 256, 256), 256)
        return lax.dot_general(
            left[which], right[which, :, cols], (((0,), (0,)), ((), ())),
            preferred_element_type=F32,
        )

    for half in range(2):
        g = grad(sib, half)
        g_sib[2 * half] = g[:, :128]
        g_sib[2 * half + 1] = g[:, 128:]
        send(g_sib.at[pl.ds(2 * half, 2)], g_recv.at[pl.ds(2 * half, 2)], 1 + half, sibling)

    take(emb_recv.at[pl.ds(0, Z * C - 1)], 0)
    total = emb_recv[0].astype(F32)
    for k in range(1, Z * C):
        total += emb_recv[k].astype(F32)
    merged[share(z, c)] = total
    for d in range(1, Z):
        send(merged.at[share(z, c)], merged.at[share(z, c)], 3, at_z(d))

    for half in range(2):
        g = grad(c, half)
        g_own[2 * half] = g[:, :128]
        g_own[2 * half + 1] = g[:, 128:]

    take(g_recv.at[pl.ds(0, 2)], 1)
    g_own[0:2] = g_own[0:2] + g_recv[0:2]
    for d in range(1, X):
        rows = pl.ds(pl.multiple_of(lax.rem(x + d, X) * 128, 128), 128)
        send(g_own.at[pl.ds(0, 2), rows], r1x.at[d - 1], 4, at_x(d))
    take(g_recv.at[pl.ds(2, 2)], 2)
    g_own[2:4] = g_own[2:4] + g_recv[2:4]
    for d in range(1, Y):
        rows = pl.ds(pl.multiple_of(lax.rem(y + d, Y) * 64, 64), 64)
        send(g_own.at[2, rows], r1y.at[d - 1], 5, at_y(d))
        rows = pl.ds(pl.multiple_of(lax.rem(z + d, Z) * 64, 64), 64)
        send(g_own.at[3, rows], r1z.at[d - 1], 6, at_z(d))

    half_rows = pl.ds(pl.multiple_of(c * (ROWS // 2), ROWS // 2), ROWS // 2)
    take(merged.at[pl.ds(0, SHARE * (Z - 1))], 3)
    send(merged.at[half_rows], merged.at[half_rows], 7, sibling)

    def summed(ref, n, first):
        for k in range(n):
            first = first + ref[k]
        return first

    take(r1x, 4)
    own = pl.ds(pl.multiple_of(x * 128, 128), 128)
    s = summed(r1x, X - 1, g_own[0:2, own])
    t2y[:, 0:16] = s[0].reshape(Y, 16, 128)
    t2z[:, 0:16] = s[1].reshape(Z, 16, 128)
    take(r1y, 5)
    s = summed(r1y, Y - 1, g_own[2, pl.ds(pl.multiple_of(y * 64, 64), 64)])
    t2z[:, 16:24] = s.reshape(Z, 8, 128)
    for d in range(1, Z):
        send(t2z.at[lax.rem(z + d, Z)], r2z.at[d - 1], 8, at_z(d))
    take(r1z, 6)
    s = summed(r1z, Z - 1, g_own[3, pl.ds(pl.multiple_of(z * 64, 64), 64)])
    t2y[:, 16:24] = s.reshape(Y, 8, 128)
    for d in range(1, Y):
        send(t2y.at[lax.rem(y + d, Y)], r2y.at[d - 1], 9, at_y(d))

    take(merged.at[half_rows], 7)
    lane = lax.broadcasted_iota(jnp.int32, (BLOCK_ROWS, 128), 1)
    squares = jnp.zeros((BLOCK_ROWS, 128), F32)
    for b in range(BLOCKS):
        m = merged[pl.ds(b * BLOCK_ROWS, BLOCK_ROWS)]
        squares = jnp.where(lane == b, jnp.sum(m * m, axis=1, keepdims=True), squares)
    emb_part = jnp.sum(squares)
    squares = squares * (1.0 / EMB)
    squares_row = jnp.transpose(squares)[0:BLOCKS]
    state_row = state_ref[...]
    state_col = jnp.transpose(
        jnp.concatenate([state_row, jnp.zeros((BLOCK_ROWS - BLOCKS, 128), F32)], axis=0)
    )

    take(r2z, 8)
    s_z = summed(r2z, Z - 1, t2z[z])
    r3y[y] = s_z[0:16]
    for d in range(1, Y):
        send(r3y.at[y], r3y.at[y], 10, at_y(d))
    take(r2y, 9)
    s_y = summed(r2y, Y - 1, t2y[y])
    r3z[z] = s_y[0:16]
    for d in range(1, Z):
        send(r3z.at[z], r3z.at[z], 11, at_z(d))
    r3x[x, 0:8] = s_y[16:24]
    r3x[x, 8:16] = s_z[16:24]
    for d in range(1, X):
        send(r3x.at[x], r3x.at[x], 12, at_x(d))

    take(r3x.at[pl.ds(0, X - 1)], 12)
    both = summed(r3x, X, 0.0)
    w4y[y, 16:24] = both[0:8]
    w4z[z, 16:24] = both[8:16]
    w4y[y, 24:32] = jnp.full((8, 128), emb_part, F32)
    take(r3y.at[pl.ds(0, Y - 1)], 10)
    w4z[z, 0:16] = summed(r3y, Y, 0.0)
    for d in range(1, Z):
        send(w4z.at[z], w4z.at[z], 13, at_z(d))
    take(r3z.at[pl.ds(0, Z - 1)], 11)
    w4y[y, 0:16] = summed(r3z, Z, 0.0)
    for d in range(1, Y):
        send(w4y.at[y], w4y.at[y], 14, at_y(d))

    take(w4z.at[pl.ds(0, Z - 1)], 13)
    f5y[c, y] = w4z[:, 16:24].reshape(64, 128)
    for d in range(1, Y):
        send(f5y.at[c, y], f5y.at[c, y], 15, at_y(d))
    f5x[c, x, 128:256] = w4z[:, 0:16].reshape(128, 128)
    take(w4y.at[pl.ds(0, Y - 1)], 14)
    f5x[c, x, 0:128] = w4y[:, 0:16].reshape(128, 128)
    f5x[c, x, 256:264] = jnp.sum(w4y[:, 24:32], axis=0)
    for d in range(1, X):
        send(f5x.at[c, x], f5x.at[c, x], 16, at_x(d))
    f5z[c, z] = w4y[:, 16:24].reshape(64, 128)
    for d in range(1, Z):
        send(f5z.at[c, z], f5z.at[c, z], 17, at_z(d))

    take(f5y.at[0, pl.ds(0, Y - 1)], 15)
    send(f5y.at[c], f5y.at[c], 18, sibling)
    take(f5x.at[0, pl.ds(0, X - 1)], 16)
    send(f5x.at[c], f5x.at[c], 19, sibling)
    take(f5z.at[0, pl.ds(0, Z - 1)], 17)
    send(f5z.at[c], f5z.at[c], 20, sibling)
    loads[5].wait()
    take(f5y.at[0], 18)
    take(f5x.at[0], 19)
    take(f5z.at[0], 20)

    squared = jnp.zeros((64, 128), F32)
    for core in range(C):
        for k in range(Y):
            v = f5y[core, k]
            squared += v * v
            v = f5z[core, k]
            squared += v * v
        for k in range(X):
            for q in range(4):
                v = f5x[core, k, 64 * q:64 * q + 64]
                squared += v * v
    emb_total = f5x[0, 0, 256:257, 0:1]
    for k in range(1, X):
        emb_total = emb_total + f5x[0, k, 256:257, 0:1]
    total = jnp.sum(squared, keepdims=True) + emb_total
    clip = jnp.minimum(1.0, 1.0 / (jnp.sqrt(total) + 1e-06))

    rate = MLP_RATE * clip
    for core, (w, out) in enumerate(((w1, new_first), (w2, new_second))):
        for q in range(2):
            cols = pl.ds(128 * q, 128)
            for k in range(X):
                rows = pl.ds(128 * k, 128)
                g = f5x[core, k, 128 * q:128 * q + 128]
                out[rows, cols] = (w[rows, cols].astype(F32) - rate * g).astype(BF16)
        for q, ref in ((2, f5y), (3, f5z)):
            cols = pl.ds(128 * q, 128)
            g = ref[core].reshape(HID, 128)
            out[:, cols] = (w[:, cols].astype(F32) - rate * g).astype(BF16)
    clip_sq = clip * clip
    new_state[...] = state_row + clip_sq * squares_row
    scale = (EMB_RATE * clip) / jnp.sqrt(state_col + clip_sq * squares)
    for b in range(BLOCKS):
        rows = pl.ds(b * BLOCK_ROWS, BLOCK_ROWS)
        new_table[rows] = table[rows] - merged[rows] * scale[:, b:b + 1]

    sent(emb_recv.at[pl.ds(0, Z * C - 1)], 0)
    sent(g_recv.at[pl.ds(0, 2)], 1)
    sent(g_recv.at[pl.ds(2, 2)], 2)
    sent(merged.at[pl.ds(0, SHARE * (Z - 1))], 3)
    sent(r1x, 4)
    sent(r1y, 5)
    sent(r1z, 6)
    sent(merged.at[half_rows], 7)
    sent(r2z, 8)
    sent(r2y, 9)
    sent(r3y.at[pl.ds(0, Y - 1)], 10)
    sent(r3z.at[pl.ds(0, Z - 1)], 11)
    sent(r3x.at[pl.ds(0, X - 1)], 12)
    sent(w4z.at[pl.ds(0, Z - 1)], 13)
    sent(w4y.at[pl.ds(0, Y - 1)], 14)
    sent(f5y.at[0, pl.ds(0, Y - 1)], 15)
    sent(f5x.at[0, pl.ds(0, X - 1)], 16)
    sent(f5z.at[0, pl.ds(0, Z - 1)], 17)
    sent(f5y.at[0], 18)
    sent(f5x.at[0], 19)
    sent(f5z.at[0], 20)


def on_device(
    table, row_state, lookup_grads, lookup_slots, lookup_rows, block_ids, block_counts,
    inputs, cotangent, w_first, w_second,
):
    vmem = pl.BlockSpec(memory_space=pltpu.VMEM)
    smem = pl.BlockSpec(memory_space=pltpu.SMEM)
    hbm = pl.BlockSpec(memory_space=pl.ANY)
    new_table, new_state, new_first, new_second = pl.pallas_call(
        kernel,
        out_shape=(
            jax.ShapeDtypeStruct((ROWS, EMB), F32),
            jax.ShapeDtypeStruct((BLOCKS, BLOCK_ROWS), F32),
            jax.ShapeDtypeStruct((HID, HID), BF16),
            jax.ShapeDtypeStruct((HID, HID), BF16),
        ),
        in_specs=[hbm, vmem, hbm, vmem, vmem, smem, smem, hbm, hbm, hbm, hbm],
        out_specs=(vmem, vmem, vmem, vmem),
        scratch_shapes=[
            pltpu.VMEM((ROWS, EMB), F32),
            pltpu.VMEM((LOOKUPS, EMB), BF16),
            pltpu.VMEM((HID, HID), BF16),
            pltpu.VMEM((HID, HID), BF16),
            pltpu.VMEM((2, SAMPLES, HID), BF16),
            pltpu.VMEM((2, SAMPLES, HID), BF16),
            pltpu.VMEM((ROWS, EMB), BF16),
            pltpu.VMEM((Z * C, SHARE, EMB), BF16),
            pltpu.VMEM((ROWS, EMB), F32),
            pltpu.VMEM((4, HID, 128), F32),
            pltpu.VMEM((4, HID, 128), F32),
            pltpu.VMEM((4, HID, 128), F32),
            pltpu.VMEM((X - 1, 2, 128, 128), F32),
            pltpu.VMEM((Y - 1, 64, 128), F32),
            pltpu.VMEM((Z - 1, 64, 128), F32),
            pltpu.VMEM((Y, 24, 128), F32),
            pltpu.VMEM((Z, 24, 128), F32),
            pltpu.VMEM((Y - 1, 24, 128), F32),
            pltpu.VMEM((Z - 1, 24, 128), F32),
            pltpu.VMEM((X, 16, 128), F32),
            pltpu.VMEM((Y, 16, 128), F32),
            pltpu.VMEM((Z, 16, 128), F32),
            pltpu.VMEM((Y, 32, 128), F32),
            pltpu.VMEM((Z, 24, 128), F32),
            pltpu.VMEM((C, X, 264, 128), F32),
            pltpu.VMEM((C, Y, 64, 128), F32),
            pltpu.VMEM((C, Z, 64, 128), F32),
            pltpu.SemaphoreType.DMA((6,)),
            pltpu.SemaphoreType.DMA((21,)),
            pltpu.SemaphoreType.DMA((21,)),
        ],
        compiler_params=pltpu.CompilerParams(
            collective_id=0, has_side_effects=True, vmem_limit_bytes=48 * 2**20
        ),
        cost_estimate=pl.CostEstimate(
            flops=2_400_000_000, bytes_accessed=6 * 2**20, transcendentals=2**20
        ),
        name="step",
    )(
        table, row_state.reshape(BLOCKS, BLOCK_ROWS), lookup_grads, lookup_slots, lookup_rows,
        block_ids, block_counts, inputs, cotangent, w_first, w_second,
    )
    return (new_table, new_state.reshape(ROWS), new_first, new_second)


def solution(mesh):
    placed = (
        P("table", None),
        P("table"),
        P("replica", "table", None),
        P("replica", "table"),
        P("replica", "table"),
        P("replica", "table"),
        P("replica", "table"),
        P(("replica", "table"), None),
        P(("replica", "table"), None),
        P(),
        P(),
    )
    return jax.shard_map(
        on_device,
        mesh=mesh,
        in_specs=placed,
        out_specs=(P("table", None), P("table"), P(), P()),
        check_vma=False,
    )
```

time: 547 us -> 82.3 us (0.15)
  waiting for transfers between devices: 394 us -> 0 us
  blocking collectives: 96.4 us -> 0 us
  Pallas kernels: 0 us -> 68.3 us
  between operations: 17.6 us -> 1.31 us
  other arithmetic: 15 us -> 0 us
  matrix products: 12.5 us -> 0 us
    psum x2 -> x0, waiting for transfers between devices: 393 us -> none  [the longest x1 283 us: on_device(): lax.psum((grad_first, grad_second), ('replica', 'table'))]
    psum x1 -> x0, blocking collectives: 96.4 us -> none  [on_device(): emb_total, mlp_total = lax.psum((emb_part, mlp_part), ('replica', 'table'))]
    pallas_call x0 -> x1, Pallas kernels: none -> 68.3 us  [on_device(): pl.pallas_call(kernel, out_shape=(jax.ShapeDtypeStruct((ROWS, EMB), F32),...]
    dot_general x5 -> x0, matrix products: 12.5 us -> none  [the longest x1 4.03 us: on_device(): jnp.einsum('bi,bj->ij', inputs, d_pre, preferred_element_type=jnp.float32)]
    reduce_sum x4 -> x0, other arithmetic: 7.22 us -> none  [the longest x1 2.1 us: on_device(): jnp.sum(grad_second * grad_second)]
    unnamed x20 -> x24, local copies, waits for them, and re-layouts: 7.26 us -> 12.2 us
  transfers between devices with their start and end apart: 2 -> 0, of which waited for: 2 -> 0; matrix products, arithmetic and copies ran while one was open for 2% -> 0% of each run, Pallas kernels for 0% -> 0%
where the time goes in v1:
time: 82.3 us; the launch traced here: 81.8 us
  Pallas kernels  68.3 us (83%)
  local copies, waits for them, and re-layouts  12.2 us (15%)
  between operations  1.31 us (2%)
    pallas_call x1, Pallas kernels, on_device(): pl.pallas_call(kernel, out_shape=(jax.ShapeDtypeStruct((ROWS, EMB), F32),...  68.3 us
    unnamed x24, local copies, waits for them, and re-layouts  12.2 us

profile of v1, /device:TPU:1, one launch (start us, length us, event | category | flops | bytes accessed | tf_op | source)
XLA Modules:
  0.0 81.8 jit_solution(5948562438663511681)
XLA Ops:
  1.3 0.0 copy-start.9
  1.3 0.6 copy-done.9
  1.9 0.0 copy-start
  1.9 1.2 %copy-done = bf16[1024,512]{1,0:T(8,128)(2,1)S(1)} copy-done((bf16[1024,512]{1,0:T(8,128)(2,1)S(1)}, bf16[1024,512]{1,0:T(8,128)(2,1)}, u32[]{:S(2)}) %copy-start) | copy-done | bytes 1048600
  3.2 0.0 copy-start.1
  3.2 1.2 %copy-done.1 = bf16[1024,512]{1,0:T(8,128)(2,1)S(1)} copy-done((bf16[1024,512]{1,0:T(8,128)(2,1)S(1)}, bf16[1024,512]{1,0:T(8,128)(2,1)}, u32[]{:S(2)}) %copy-start.1) | copy-done | bytes 1048600
  4.4 0.0 copy-start.2
  4.4 1.0 %copy-done.2 = f32[1024,128]{1,0:T(8,128)S(1)} copy-done((f32[1024,128]{1,0:T(8,128)S(1)}, f32[1024,128]{1,0:T(8,128)}, u32[]{:S(2)}) %copy-start.2) | copy-done | bytes 524312
  5.4 0.0 copy-start.3
  5.4 1.0 %copy-done.3 = bf16[512,512]{1,0:T(8,128)(2,1)S(1)} copy-done((bf16[512,512]{1,0:T(8,128)(2,1)S(1)}, bf16[512,512]{1,0:T(8,128)(2,1)}, u32[]{:S(2)}) %copy-start.3) | copy-done | bytes 524312
  6.5 0.0 copy-start.4
  6.5 1.0 %copy-done.4 = bf16[512,512]{1,0:T(8,128)(2,1)S(1)} copy-done((bf16[512,512]{1,0:T(8,128)(2,1)S(1)}, bf16[512,512]{1,0:T(8,128)(2,1)}, u32[]{:S(2)}) %copy-start.4) | copy-done | bytes 524312
  7.5 0.0 copy-start.5
  7.5 0.9 %copy-done.5 = bf16[1,1024,128]{2,1,0:T(8,128)(2,1)S(1)} copy-done((bf16[1,1024,128]{2,1,0:T(8,128)(2,1)S(1)}, bf16[1,1024,128]{2,1,0:T(8,128)(2,1)}, u32[]{:S(2)}) %copy-start.5) | copy-done | bytes 262168
  8.5 0.0 copy-start.6
  8.5 0.7 copy-done.6
  9.2 0.0 copy-start.7
  9.2 0.7 copy-done.7
  9.8 0.0 copy-start.8
  9.8 0.7 copy-done.8
  10.5 68.3 %step.1 = (f32[1024,128]{1,0:T(8,128)S(1)}, f32[8,128]{1,0:T(8,128)S(1)}, bf16[512,512]{1,0:T(8,128)(2,1)S(1)}, bf16[512,512]{1,0:T(8,128)(2,1)S(1)}) custom-call(f32[1024,128]{1,0:T(8,128)S(1)} %copy-done.2, f32[8,128]{1,0:T(8,128)S(1)} %bitcast.3, bf16[1,1024,128]{2,1,0:T(8,128)(2,1)S(1)} %copy-done.5, s32[1,1024]{1,0:T(1,128)S(1)} %copy-done.7, ...), custom_call_target="tpu_custom_call" | custom-call | flops 2400000000 | bytes 6291456 | tf_op jit(solution)/shard_map/step/pallas_call | solution.py:326
  78.9 0.8 copy.20
  79.7 0.6 copy.21
  80.2 0.8 copy.22
  81.0 0.8 copy.23
Async XLA Ops:
  1.3 0.7 copy-start.9
  1.9 1.2 %copy-start = (bf16[1024,512]{1,0:T(8,128)(2,1)S(1)}, bf16[1024,512]{1,0:T(8,128)(2,1)}, u32[]{:S(2)}) copy-start(bf16[1024,512]{1,0:T(8,128)(2,1)} %inputs_hbm.1) | copy-start | bytes 3145732
  3.2 1.2 %copy-start.1 = (bf16[1024,512]{1,0:T(8,128)(2,1)S(1)}, bf16[1024,512]{1,0:T(8,128)(2,1)}, u32[]{:S(2)}) copy-start(bf16[1024,512]{1,0:T(8,128)(2,1)} %cot_hbm.1) | copy-start | bytes 3145732
  4.4 1.0 %copy-start.2 = (f32[1024,128]{1,0:T(8,128)S(1)}, f32[1024,128]{1,0:T(8,128)}, u32[]{:S(2)}) copy-start(f32[1024,128]{1,0:T(8,128)} %table_hbm.1) | copy-start | bytes 1572868
  5.4 1.0 %copy-start.3 = (bf16[512,512]{1,0:T(8,128)(2,1)S(1)}, bf16[512,512]{1,0:T(8,128)(2,1)}, u32[]{:S(2)}) copy-start(bf16[512,512]{1,0:T(8,128)(2,1)} %w1_hbm.1) | copy-start | bytes 1572868
  6.5 1.0 %copy-start.4 = (bf16[512,512]{1,0:T(8,128)(2,1)S(1)}, bf16[512,512]{1,0:T(8,128)(2,1)}, u32[]{:S(2)}) copy-start(bf16[512,512]{1,0:T(8,128)(2,1)} %w2_hbm.1) | copy-start | bytes 1572868
  7.5 0.9 %copy-start.5 = (bf16[1,1024,128]{2,1,0:T(8,128)(2,1)S(1)}, bf16[1,1024,128]{2,1,0:T(8,128)(2,1)}, u32[]{:S(2)}) copy-start(bf16[1,1024,128]{2,1,0:T(8,128)(2,1)} %grads_hbm.1) | copy-start | bytes 786436
  8.5 0.7 copy-start.6
  9.2 0.7 copy-start.7
  9.8 0.7 copy-start.8

commit v2 on v1

v2 whole, which is shorter than its diff:
```python
import jax
import jax.numpy as jnp
from jax import lax
from jax.experimental import pallas as pl
from jax.experimental.pallas import tpu as pltpu
from jax.sharding import PartitionSpec as P

X, Y, Z, C = 4, 8, 8, 2
BLOCK_ROWS = 128
EMB = 128
HID = 512
SLOTS = 4
BLOCKS = 8
SAMPLES = 1024
LOOKUPS = 1024
ROWS = BLOCKS * BLOCK_ROWS
SHARE = ROWS // (Z * C)
CHUNK = 256
FAR = {4: (2, 1, 3), 8: (4, 3, 5, 2, 6, 1, 7)}

EMB_RATE = 0.05
MLP_RATE = 0.04 * HID
F32 = jnp.float32
BF16 = jnp.bfloat16
MESH = pl.DeviceIdType.MESH


def kernel(
    table_hbm, state_hbm, grads_hbm, slots_hbm, rows_hbm, ids_hbm, count_hbm,
    inputs_hbm, cot_hbm, w1_hbm, w2_hbm,
    new_table, new_state, new_first, new_second,
    table, state_ref, lgrads, slots_ref, rows_ref, ids_ref, count_ref, w1, w2, left, right,
    dense, emb_recv, merged,
    g_sib, g_own, g_recv,
    r1x, r1y, r1z, t2y, t2z, r2y, r2z, r3x, r3y, r3z, w4y, w4z, f5x, f5y, f5z,
    in_sem, out_sem, send_sem, recv_sem,
):
    rep = lax.axis_index("replica")
    tab = lax.axis_index("table")
    z, c = rep // C, lax.rem(rep, C)
    x, y = tab // Y, lax.rem(tab, Y)
    sib = 1 - c

    def at_x(d):
        return (rep, lax.rem(x + d, X) * Y + y)

    def at_y(d):
        return (rep, x * Y + lax.rem(y + d, Y))

    def at_z(d, core=c):
        return (lax.rem(z + d, Z) * C + core, tab)

    sibling = (z * C + sib, tab)

    opened, taken = {}, set()

    def send(src, dst, k, dev, whole):
        opened[k] = whole
        pltpu.make_async_remote_copy(
            src_ref=src, dst_ref=dst, send_sem=send_sem.at[k], recv_sem=recv_sem.at[k],
            device_id=dev, device_id_type=MESH,
        ).start()

    def take(k):
        taken.add(k)
        pltpu.make_async_copy(opened[k], opened[k], recv_sem.at[k]).wait()

    def finish():
        for k, whole in opened.items():
            if k not in taken:
                take(k)
            pltpu.make_async_copy(whole, whole, send_sem.at[k]).wait()

    parts = [pl.ds(k * CHUNK, CHUNK) for k in range(SAMPLES // CHUNK)]
    pairs = [
        (count_hbm, count_ref), (ids_hbm, ids_ref), (slots_hbm, slots_ref), (rows_hbm, rows_ref),
        (grads_hbm.at[0], lgrads), (w1_hbm, w1), (w2_hbm, w2),
    ]
    for rows in parts:
        pairs += [(inputs_hbm.at[rows], left.at[0, rows]), (cot_hbm.at[rows], right.at[1, rows])]
    pairs += [(state_hbm, state_ref), (table_hbm, table)]
    loads = [pltpu.make_async_copy(*pair, in_sem.at[k]) for k, pair in enumerate(pairs)]
    for load in loads:
        load.start()

    barrier = pltpu.get_barrier_semaphore()
    peers = [at_x(d) for d in range(1, X)] + [at_y(d) for d in range(1, Y)]
    peers += [at_z(d) for d in range(1, Z)] + [at_z(d, sib) for d in range(Z)]
    for dev in peers:
        pl.semaphore_signal(barrier, inc=1, device_id=dev, device_id_type=MESH)

    for load in loads[:5]:
        load.wait()
    count = count_ref[0, 0]
    slot_ids = slots_ref[...]
    position = jnp.where(slot_ids < count, slot_ids * BLOCK_ROWS + rows_ref[...], -1)
    lookup_grads = lgrads[...]
    slot_sums = []
    for k in range(SLOTS):
        target = lax.broadcasted_iota(jnp.int32, (BLOCK_ROWS, LOOKUPS), 0) + k * BLOCK_ROWS
        onehot = jnp.where(target == position, 1.0, 0.0).astype(BF16)
        summed = jnp.dot(onehot, lookup_grads, preferred_element_type=F32)
        slot_sums.append(summed.astype(BF16).astype(F32))
    for b in range(BLOCKS):
        block = jnp.zeros((BLOCK_ROWS, EMB), F32)
        for k in range(SLOTS):
            block += jnp.where((ids_ref[0, k] == b) & (k < count), 1.0, 0.0) * slot_sums[k]
        dense[pl.ds(b * BLOCK_ROWS, BLOCK_ROWS)] = block.astype(BF16)

    def share(zz, cc):
        return pl.ds(pl.multiple_of((cc * Z + zz) * SHARE, SHARE), SHARE)

    loads[5].wait()
    loads[6].wait()
    for k, rows in enumerate(parts):
        loads[7 + 2 * k].wait()
        loads[8 + 2 * k].wait()
        pre = jnp.dot(left[0, rows], w1[...], preferred_element_type=F32)
        back = lax.dot_general(
            right[1, rows], w2[...], (((1,), (1,)), ((), ())), preferred_element_type=F32
        )
        sig = jax.nn.sigmoid(pre)
        left[1, rows] = (pre * sig).astype(BF16)
        right[0, rows] = (back * sig * (1.0 + pre * (1.0 - sig))).astype(BF16)

    def grad(which, half):
        cols = pl.ds(half * 256, 256)
        return lax.dot_general(
            left[which], right[which, :, cols], (((0,), (0,)), ((), ())),
            preferred_element_type=F32,
        )

    pl.semaphore_wait(barrier, len(peers))
    for half in (1, 0):
        g = grad(sib, half)
        g_sib[2 * half] = g[:, :128]
        g_sib[2 * half + 1] = g[:, 128:]
        two = pl.ds(2 * half, 2)
        send(g_sib.at[two], g_recv.at[two], 1 + half, sibling, g_recv.at[two])
    for half in (1, 0):
        g = grad(c, half)
        g_own[2 * half] = g[:, :128]
        g_own[2 * half + 1] = g[:, 128:]

    for d in FAR[Z] + (0,):
        for core in (c, sib):
            if d == 0 and core is c:
                continue
            send(
                dense.at[share(lax.rem(z + d, Z), core)], emb_recv.at[rep], 0, at_z(d, core),
                emb_recv.at[pl.ds(0, Z * C - 1)],
            )
    emb_recv[rep] = dense[share(z, c)]

    take(2)
    g_own[2:4] = g_own[2:4] + g_recv[2:4]
    for d in FAR[Y]:
        rows = pl.ds(pl.multiple_of(lax.rem(y + d, Y) * 64, 64), 64)
        send(g_own.at[2, rows], r1y.at[d - 1], 5, at_y(d), r1y)
        rows = pl.ds(pl.multiple_of(lax.rem(z + d, Z) * 64, 64), 64)
        send(g_own.at[3, rows], r1z.at[d - 1], 6, at_z(d), r1z)
    take(1)
    g_own[0:2] = g_own[0:2] + g_recv[0:2]
    for d in FAR[X]:
        rows = pl.ds(pl.multiple_of(lax.rem(x + d, X) * 128, 128), 128)
        send(g_own.at[pl.ds(0, 2), rows], r1x.at[d - 1], 4, at_x(d), r1x)

    def summed(ref, n, first):
        for k in range(n):
            first = first + ref[k]
        return first

    take(4)
    own = pl.ds(pl.multiple_of(x * 128, 128), 128)
    s = summed(r1x, X - 1, g_own[0:2, own])
    t2y[:, 0:16] = s[0].reshape(Y, 16, 128)
    t2z[:, 0:16] = s[1].reshape(Z, 16, 128)
    take(5)
    s = summed(r1y, Y - 1, g_own[2, pl.ds(pl.multiple_of(y * 64, 64), 64)])
    t2z[:, 16:24] = s.reshape(Z, 8, 128)
    for d in FAR[Z]:
        send(t2z.at[lax.rem(z + d, Z)], r2z.at[d - 1], 8, at_z(d), r2z)
    take(6)
    s = summed(r1z, Z - 1, g_own[3, pl.ds(pl.multiple_of(z * 64, 64), 64)])
    t2y[:, 16:24] = s.reshape(Y, 8, 128)
    for d in FAR[Y]:
        send(t2y.at[lax.rem(y + d, Y)], r2y.at[d - 1], 9, at_y(d), r2y)

    take(0)
    total = emb_recv[0].astype(F32)
    for k in range(1, Z * C):
        total += emb_recv[k].astype(F32)
    merged[share(z, c)] = total
    for d in FAR[Z]:
        send(
            merged.at[share(z, c)], merged.at[share(z, c)], 3, at_z(d),
            merged.at[pl.ds(0, SHARE * (Z - 1))],
        )

    take(8)
    s_z = summed(r2z, Z - 1, t2z[z])
    r3y[y] = s_z[0:16]
    for d in FAR[Y]:
        send(r3y.at[y], r3y.at[y], 10, at_y(d), r3y.at[pl.ds(0, Y - 1)])
    take(9)
    s_y = summed(r2y, Y - 1, t2y[y])
    r3z[z] = s_y[0:16]
    for d in FAR[Z]:
        send(r3z.at[z], r3z.at[z], 11, at_z(d), r3z.at[pl.ds(0, Z - 1)])
    r3x[x, 0:8] = s_y[16:24]
    r3x[x, 8:16] = s_z[16:24]
    for d in FAR[X]:
        send(r3x.at[x], r3x.at[x], 12, at_x(d), r3x.at[pl.ds(0, X - 1)])

    half_rows = pl.ds(pl.multiple_of(c * (ROWS // 2), ROWS // 2), ROWS // 2)
    take(3)
    send(merged.at[half_rows], merged.at[half_rows], 7, sibling, merged.at[half_rows])
    lane = lax.broadcasted_iota(jnp.int32, (BLOCK_ROWS, 128), 1)

    def squares_of(core):
        found = jnp.zeros((BLOCK_ROWS, 128), F32)
        for k in range(BLOCKS // C):
            b = core * (BLOCKS // C) + k
            m = merged[pl.ds(pl.multiple_of(b * BLOCK_ROWS, BLOCK_ROWS), BLOCK_ROWS)]
            found = jnp.where(lane == b, jnp.sum(m * m, axis=1, keepdims=True), found)
        return found

    squares = squares_of(c)
    emb_part = jnp.sum(squares)

    take(12)
    both = summed(r3x, X, 0.0)
    w4y[y, 16:24] = both[0:8]
    w4z[z, 16:24] = both[8:16]
    w4y[y, 24:32] = jnp.full((8, 128), emb_part, F32)
    take(10)
    w4z[z, 0:16] = summed(r3y, Y, 0.0)
    for d in FAR[Z]:
        send(w4z.at[z], w4z.at[z], 13, at_z(d), w4z.at[pl.ds(0, Z - 1)])
    take(11)
    w4y[y, 0:16] = summed(r3z, Z, 0.0)
    for d in FAR[Y]:
        send(w4y.at[y], w4y.at[y], 14, at_y(d), w4y.at[pl.ds(0, Y - 1)])

    take(7)
    squares = (squares + squares_of(sib)) * (1.0 / EMB)
    squares_row = jnp.transpose(squares)[0:BLOCKS]
    loads[-2].wait()
    state_row = state_ref[...]
    state_col = jnp.transpose(
        jnp.concatenate([state_row, jnp.zeros((BLOCK_ROWS - BLOCKS, 128), F32)], axis=0)
    )

    take(13)
    f5y[c, y] = w4z[:, 16:24].reshape(64, 128)
    for d in FAR[Y]:
        send(f5y.at[c, y], f5y.at[c, y], 15, at_y(d), f5y.at[0, pl.ds(0, Y - 1)])
    f5x[c, x, 128:256] = w4z[:, 0:16].reshape(128, 128)
    take(14)
    f5z[c, z] = w4y[:, 16:24].reshape(64, 128)
    for d in FAR[Z]:
        send(f5z.at[c, z], f5z.at[c, z], 17, at_z(d), f5z.at[0, pl.ds(0, Z - 1)])
    f5x[c, x, 0:128] = w4y[:, 0:16].reshape(128, 128)
    f5x[c, x, 256:264] = jnp.sum(w4y[:, 24:32], axis=0)
    for d in FAR[X]:
        send(f5x.at[c, x], f5x.at[c, x], 16, at_x(d), f5x.at[0, pl.ds(0, X - 1)])

    def squared(core, ref, n, rows):
        found = jnp.zeros((64, 128), F32)
        for k in range(n):
            for q in range(rows // 64):
                v = ref[core, k, 64 * q:64 * q + 64]
                found += v * v
        return found

    def emb_of(core):
        found = f5x[core, 0, 256:264]
        for k in range(1, X):
            found = found + f5x[core, k, 256:264]
        return found[0:1, 0:1]

    take(15)
    send(f5y.at[c], f5y.at[c], 18, sibling, f5y.at[0])
    take(17)
    send(f5z.at[c], f5z.at[c], 20, sibling, f5z.at[0])
    take(16)
    send(f5x.at[c], f5x.at[c], 19, sibling, f5x.at[0])
    mine = squared(c, f5y, Y, 64) + squared(c, f5z, Z, 64) + squared(c, f5x, X, 256)
    loads[-1].wait()
    take(18)
    take(20)
    take(19)
    other = squared(sib, f5y, Y, 64) + squared(sib, f5z, Z, 64) + squared(sib, f5x, X, 256)

    total = jnp.sum(mine + other, keepdims=True) + (emb_of(c) + emb_of(sib))
    clip = jnp.minimum(1.0, 1.0 / (jnp.sqrt(total) + 1e-06))

    def store(src, dst, k):
        copy = pltpu.make_async_copy(src, dst, out_sem.at[k])
        copy.start()
        return copy

    clip_sq = clip * clip
    scale = (EMB_RATE * clip) / jnp.sqrt(state_col + clip_sq * squares)
    for b in range(BLOCKS):
        rows = pl.ds(b * BLOCK_ROWS, BLOCK_ROWS)
        table[rows] = table[rows] - merged[rows] * scale[:, b:b + 1]
    stores = [store(table, new_table, 0)]
    state_ref[...] = state_row + clip_sq * squares_row
    stores.append(store(state_ref, new_state, 1))
    rate = MLP_RATE * clip
    for core, (w, out) in enumerate(((w1, new_first), (w2, new_second))):
        for q in range(2):
            cols = pl.ds(128 * q, 128)
            for k in range(X):
                rows = pl.ds(128 * k, 128)
                g = f5x[core, k, 128 * q:128 * q + 128]
                w[rows, cols] = (w[rows, cols].astype(F32) - rate * g).astype(BF16)
        for q, ref in ((2, f5y), (3, f5z)):
            cols = pl.ds(128 * q, 128)
            g = ref[core].reshape(HID, 128)
            w[:, cols] = (w[:, cols].astype(F32) - rate * g).astype(BF16)
        stores.append(store(w, out, 2 + core))
    finish()
    for copy in stores:
        copy.wait()


def hand_over(*refs):
    n = len(refs) // 3
    arrays, held, sem = refs[: 2 * n], refs[2 * n : 3 * n], refs[-1]
    loads = [pltpu.make_async_copy(arrays[k], held[k], sem.at[k]) for k in range(n)]
    stores = [pltpu.make_async_copy(held[k], arrays[n + k], sem.at[n + k]) for k in range(n)]
    for load in loads:
        load.start()
    for load, store in zip(loads, stores):
        load.wait()
        store.start()
    for store in stores:
        store.wait()


def on_device(
    table, row_state, lookup_grads, lookup_slots, lookup_rows, block_ids, block_counts,
    inputs, cotangent, w_first, w_second,
):
    hbm = pl.BlockSpec(memory_space=pl.ANY)
    shapes = (
        jax.ShapeDtypeStruct((ROWS, EMB), F32),
        jax.ShapeDtypeStruct((BLOCKS, BLOCK_ROWS), F32),
        jax.ShapeDtypeStruct((HID, HID), BF16),
        jax.ShapeDtypeStruct((HID, HID), BF16),
    )
    results = pl.pallas_call(
        kernel,
        out_shape=shapes,
        in_specs=[hbm] * 11,
        out_specs=(hbm,) * 4,
        scratch_shapes=[
            pltpu.VMEM((ROWS, EMB), F32),
            pltpu.VMEM((BLOCKS, BLOCK_ROWS), F32),
            pltpu.VMEM((LOOKUPS, EMB), BF16),
            pltpu.VMEM((1, LOOKUPS), jnp.int32),
            pltpu.VMEM((1, LOOKUPS), jnp.int32),
            pltpu.SMEM((1, SLOTS), jnp.int32),
            pltpu.SMEM((1, 1), jnp.int32),
            pltpu.VMEM((HID, HID), BF16),
            pltpu.VMEM((HID, HID), BF16),
            pltpu.VMEM((2, SAMPLES, HID), BF16),
            pltpu.VMEM((2, SAMPLES, HID), BF16),
            pltpu.VMEM((ROWS, EMB), BF16),
            pltpu.VMEM((Z * C, SHARE, EMB), BF16),
            pltpu.VMEM((ROWS, EMB), F32),
            pltpu.VMEM((4, HID, 128), F32),
            pltpu.VMEM((4, HID, 128), F32),
            pltpu.VMEM((4, HID, 128), F32),
            pltpu.VMEM((X - 1, 2, 128, 128), F32),
            pltpu.VMEM((Y - 1, 64, 128), F32),
            pltpu.VMEM((Z - 1, 64, 128), F32),
            pltpu.VMEM((Y, 24, 128), F32),
            pltpu.VMEM((Z, 24, 128), F32),
            pltpu.VMEM((Y - 1, 24, 128), F32),
            pltpu.VMEM((Z - 1, 24, 128), F32),
            pltpu.VMEM((X, 16, 128), F32),
            pltpu.VMEM((Y, 16, 128), F32),
            pltpu.VMEM((Z, 16, 128), F32),
            pltpu.VMEM((Y, 32, 128), F32),
            pltpu.VMEM((Z, 24, 128), F32),
            pltpu.VMEM((C, X, 264, 128), F32),
            pltpu.VMEM((C, Y, 64, 128), F32),
            pltpu.VMEM((C, Z, 64, 128), F32),
            pltpu.SemaphoreType.DMA((9 + 2 * SAMPLES // CHUNK,)),
            pltpu.SemaphoreType.DMA((4,)),
            pltpu.SemaphoreType.DMA((21,)),
            pltpu.SemaphoreType.DMA((21,)),
        ],
        compiler_params=pltpu.CompilerParams(
            collective_id=0, has_side_effects=True, vmem_limit_bytes=60 * 2**20
        ),
        cost_estimate=pl.CostEstimate(
            flops=2_400_000_000, bytes_accessed=6 * 2**20, transcendentals=2**20
        ),
        name="step",
    )(
        table, row_state.reshape(BLOCKS, BLOCK_ROWS), lookup_grads, lookup_slots, lookup_rows,
        block_ids, block_counts, inputs, cotangent, w_first, w_second,
    )
    new_table, new_state, new_first, new_second = pl.pallas_call(
        hand_over,
        out_shape=shapes,
        in_specs=[hbm] * 4,
        out_specs=(hbm,) * 4,
        scratch_shapes=[pltpu.VMEM(a.shape, a.dtype) for a in shapes]
        + [pltpu.SemaphoreType.DMA((8,))],
        compiler_params=pltpu.CompilerParams(vmem_limit_bytes=60 * 2**20),
        name="hand_over",
    )(*results)
    return (new_table, new_state.reshape(ROWS), new_first, new_second)


def solution(mesh):
    placed = (
        P("table", None),
        P("table"),
        P("replica", "table", None),
        P("replica", "table"),
        P("replica", "table"),
        P("replica", "table"),
        P("replica", "table"),
        P(("replica", "table"), None),
        P(("replica", "table"), None),
        P(),
        P(),
    )
    return jax.shard_map(
        on_device,
        mesh=mesh,
        in_specs=placed,
        out_specs=(P("table", None), P("table"), P(), P()),
        check_vma=False,
    )
```

time: 82.3 us -> 62.3 us (0.76)
  local copies, waits for them, and re-layouts: 12.2 us -> 0 us
  Pallas kernels: 68.3 us -> 60.8 us
    unnamed x24 -> x0, local copies, waits for them, and re-layouts: 12.2 us -> none
    pallas_call x1 -> x2, Pallas kernels: 68.3 us -> 60.8 us  [the longest x1 58.6 us: on_device(): pl.pallas_call(kernel, out_shape=shapes, in_specs=[hbm] * 11, out_specs=(...]
where the time goes in v2:
time: 62.3 us; the launch traced here: 62.1 us
  Pallas kernels  60.8 us (98%)
  between operations  1.29 us (2%)
    pallas_call x1, Pallas kernels, on_device(): pl.pallas_call(kernel, out_shape=shapes, in_specs=[hbm] * 11, out_specs=(...  58.6 us
    pallas_call x1, Pallas kernels, on_device(): pl.pallas_call(hand_over, out_shape=shapes, in_specs=[hbm] * 4, out_specs...  2.25 us

profile of v2, /device:TPU:1, one launch (start us, length us, event | category | flops | bytes accessed | tf_op | source)
XLA Modules:
  0.0 62.1 jit_solution(16321480066047585864)
XLA Ops:
  1.3 58.6 %step.1 = (f32[1024,128]{1,0:T(8,128)}, f32[8,128]{1,0:T(8,128)}, bf16[512,512]{1,0:T(8,128)(2,1)}, bf16[512,512]{1,0:T(8,128)(2,1)}) custom-call(f32[1024,128]{1,0:T(8,128)} %table_hbm.1, f32[8,128]{1,0:T(8,128)} %bitcast.2, bf16[1,1024,128]{2,1,0:T(8,128)(2,1)} %grads_hbm.1, s32[1,1024]{1,0:T(1,128)} %slots_hbm.1, s32[1,1024]{1,0:T(1,128)} %rows_hbm.1, ...), custom_call_target="tpu_custom_call" | custom-call | flops 2400000000 | bytes 6291456 | tf_op jit(solution)/shard_map/step/pallas_call | solution.py:354
  59.9 2.3 %hand_over.1 = (f32[1024,128]{1,0:T(8,128)}, f32[8,128]{1,0:T(8,128)}, bf16[512,512]{1,0:T(8,128)(2,1)}, bf16[512,512]{1,0:T(8,128)(2,1)}) custom-call(f32[1024,128]{1,0:T(8,128)} %get-tuple-element.12.refs_0_, f32[8,128]{1,0:T(8,128)} %get-tuple-element.13.refs_1_, bf16[512,512]{1,0:T(8,128)(2,1)} %get-tuple-element.14.refs_2_, ...), custom_call_target="tpu_custom_call" | custom-call | tf_op jit(solution)/shard_map/hand_over/pallas_call | solution.py:408

commit v3 on v2

v3 whole, which is shorter than its diff:
```python
import jax
import jax.numpy as jnp
from jax import lax
from jax.experimental import pallas as pl
from jax.experimental.pallas import tpu as pltpu
from jax.sharding import PartitionSpec as P

X, Y, Z, C = 4, 8, 8, 2
BLOCK_ROWS = 128
EMB = 128
HID = 512
SLOTS = 4
BLOCKS = 8
SAMPLES = 1024
LOOKUPS = 1024
ROWS = BLOCKS * BLOCK_ROWS
SHARE = ROWS // (Z * C)
CHUNK = 256
PAIR = 22
FAR = {4: (2, 1, 3), 8: (4, 3, 5, 2, 6, 1, 7)}

EMB_RATE = 0.05
MLP_RATE = 0.04 * HID
F32 = jnp.float32
BF16 = jnp.bfloat16
MESH = pl.DeviceIdType.MESH


def kernel(
    table_hbm, state_hbm, grads_hbm, slots_hbm, rows_hbm, ids_hbm, count_hbm,
    inputs_hbm, cot_hbm, w1_hbm, w2_hbm,
    new_table, new_state, new_first, new_second,
    table, state_ref, lgrads, slots_ref, rows_ref, ids_ref, count_ref, w1, w2, left, right,
    dense, emb_recv, merged,
    g_sib, g_own, g_recv,
    r1x, r1y, r1z, t2x, t2y, t2z, r2x, r2y, r2z, r3y, r3z, w4x, w4y, w4z, f5x, f5y, f5z,
    in_sem, send_sem, recv_sem,
):
    rep = lax.axis_index("replica")
    tab = lax.axis_index("table")
    z, c = rep // C, lax.rem(rep, C)
    x, y = tab // Y, lax.rem(tab, Y)
    sib = 1 - c

    def at_x(d):
        return (rep, lax.rem(x + d, X) * Y + y)

    def at_y(d):
        return (rep, x * Y + lax.rem(y + d, Y))

    def at_z(d, core=c):
        return (lax.rem(z + d, Z) * C + core, tab)

    sibling = (z * C + sib, tab)

    opened, taken = {}, set()

    def send(src, dst, k, dev, whole):
        opened[k] = whole
        pltpu.make_async_remote_copy(
            src_ref=src, dst_ref=dst, send_sem=send_sem.at[k], recv_sem=recv_sem.at[k],
            device_id=dev, device_id_type=MESH,
        ).start()

    def take(k):
        taken.add(k)
        pltpu.make_async_copy(opened[k], opened[k], recv_sem.at[k]).wait()

    def finish():
        for k, whole in opened.items():
            if k not in taken:
                take(k)
            pltpu.make_async_copy(whole, whole, send_sem.at[k]).wait()

    parts = [pl.ds(k * CHUNK, CHUNK) for k in range(SAMPLES // CHUNK)]
    pairs = [
        (count_hbm, count_ref), (ids_hbm, ids_ref), (slots_hbm, slots_ref), (rows_hbm, rows_ref),
        (grads_hbm.at[0], lgrads), (w1_hbm, w1), (w2_hbm, w2),
    ]
    for rows in parts:
        pairs += [(inputs_hbm.at[rows], left.at[0, rows]), (cot_hbm.at[rows], right.at[1, rows])]
    pairs += [(state_hbm, state_ref), (table_hbm, table)]
    loads = [pltpu.make_async_copy(*pair, in_sem.at[k]) for k, pair in enumerate(pairs)]
    for load in loads:
        load.start()

    barrier = pltpu.get_barrier_semaphore()
    peers = [at_x(d) for d in range(1, X)] + [at_y(d) for d in range(1, Y)]
    peers += [at_z(d) for d in range(1, Z)] + [at_z(d, sib) for d in range(Z)]
    for dev in peers:
        pl.semaphore_signal(barrier, inc=1, device_id=dev, device_id_type=MESH)

    for load in loads[:5]:
        load.wait()
    count = count_ref[0, 0]
    slot_ids = slots_ref[...]
    position = jnp.where(slot_ids < count, slot_ids * BLOCK_ROWS + rows_ref[...], -1)
    lookup_grads = lgrads[...]
    slot_sums = []
    for k in range(SLOTS):
        target = lax.broadcasted_iota(jnp.int32, (BLOCK_ROWS, LOOKUPS), 0) + k * BLOCK_ROWS
        onehot = jnp.where(target == position, 1.0, 0.0).astype(BF16)
        found = jnp.dot(onehot, lookup_grads, preferred_element_type=F32)
        slot_sums.append(found.astype(BF16).astype(F32))
    for b in range(BLOCKS):
        block = jnp.zeros((BLOCK_ROWS, EMB), F32)
        for k in range(SLOTS):
            block += jnp.where((ids_ref[0, k] == b) & (k < count), 1.0, 0.0) * slot_sums[k]
        dense[pl.ds(b * BLOCK_ROWS, BLOCK_ROWS)] = block.astype(BF16)

    def share(zz, cc):
        return pl.ds(pl.multiple_of((cc * Z + zz) * SHARE, SHARE), SHARE)

    pl.semaphore_wait(barrier, len(peers))
    for d in FAR[Z] + (0,):
        for core in (c, sib):
            if d == 0 and core is c:
                continue
            send(
                dense.at[share(lax.rem(z + d, Z), core)], emb_recv.at[rep], 0, at_z(d, core),
                emb_recv.at[pl.ds(0, Z * C - 1)],
            )
    emb_recv[rep] = dense[share(z, c)]

    loads[5].wait()
    loads[6].wait()
    for k, rows in enumerate(parts):
        loads[7 + 2 * k].wait()
        loads[8 + 2 * k].wait()
        pre = jnp.dot(left[0, rows], w1[...], preferred_element_type=F32)
        back = lax.dot_general(
            right[1, rows], w2[...], (((1,), (1,)), ((), ())), preferred_element_type=F32
        )
        sig = jax.nn.sigmoid(pre)
        left[1, rows] = (pre * sig).astype(BF16)
        right[0, rows] = (back * sig * (1.0 + pre * (1.0 - sig))).astype(BF16)

    def grad(which, half):
        cols = pl.ds(half * 256, 256)
        return lax.dot_general(
            left[which], right[which, :, cols], (((0,), (0,)), ((), ())),
            preferred_element_type=F32,
        )

    for half in (1, 0):
        g = grad(sib, half)
        for k in range(2):
            block = 2 * half + k
            g_sib[block] = g[:, 128 * k:128 * k + 128]
            send(g_sib.at[block], g_recv.at[block], PAIR + block, sibling, g_recv.at[block])
    for half in (1, 0):
        g = grad(c, half)
        g_own[2 * half] = g[:, :128]
        g_own[2 * half + 1] = g[:, 128:]

    def piece(k, rows):
        return pl.ds(pl.multiple_of(k * rows, rows), rows)

    take(PAIR + 2)
    g_own[2] = g_own[2] + g_recv[2]
    for d in FAR[Y]:
        send(g_own.at[2, piece(lax.rem(y + d, Y), 64)], r1y.at[d - 1], 5, at_y(d), r1y)
    take(PAIR + 3)
    g_own[3] = g_own[3] + g_recv[3]
    for d in FAR[Z]:
        send(g_own.at[3, piece(lax.rem(z + d, Z), 64)], r1z.at[d - 1], 6, at_z(d), r1z)
    take(PAIR)
    take(PAIR + 1)
    g_own[0:2] = g_own[0:2] + g_recv[0:2]
    for d in FAR[X]:
        rows = piece(lax.rem(x + d, X), 128)
        send(g_own.at[pl.ds(0, 2), rows], r1x.at[d - 1], 4, at_x(d), r1x)

    def summed(ref, n, first):
        for k in range(n):
            first = first + ref[k]
        return first

    take(0)
    total = emb_recv[0].astype(F32)
    for k in range(1, Z * C):
        total += emb_recv[k].astype(F32)
    merged[share(z, c)] = total
    r3z[z, 32:40] = jnp.sum((total * total).reshape(SHARE // 8, 8, EMB), axis=0)

    take(4)
    s = summed(r1x, X - 1, g_own[0:2, piece(x, 128)])
    t2y[...] = s[0].reshape(Y, 16, 128)
    t2z[...] = s[1].reshape(Z, 16, 128)
    for d in FAR[Y]:
        send(t2y.at[lax.rem(y + d, Y)], r2y.at[d - 1], 9, at_y(d), r2y)
        send(t2z.at[lax.rem(z + d, Z)], r2z.at[d - 1], 8, at_z(d), r2z)
    for d in (2, 6, 1, 7):
        send(
            merged.at[share(z, c)], merged.at[share(z, c)], 3, at_z(d),
            merged.at[pl.ds(0, SHARE * (Z - 1))],
        )

    take(5)
    t2x[:, 0:16] = summed(r1y, Y - 1, g_own[2, piece(y, 64)]).reshape(X, 16, 128)
    take(6)
    t2x[:, 16:32] = summed(r1z, Z - 1, g_own[3, piece(z, 64)]).reshape(X, 16, 128)
    for d in FAR[X]:
        send(t2x.at[lax.rem(x + d, X)], r2x.at[d - 1], 7, at_x(d), r2x)

    take(9)
    r3z[z, 0:16] = summed(r2y, Y - 1, t2y[y])
    take(8)
    r3y[y, 0:16] = summed(r2z, Z - 1, t2z[z])
    take(7)
    s = summed(r2x, X - 1, t2x[x])
    r3z[z, 16:32] = s[0:16]
    r3y[y, 16:32] = s[16:32]
    for d in FAR[Y]:
        send(r3z.at[z], r3z.at[z], 11, at_z(d), r3z.at[pl.ds(0, Z - 1)])
        send(r3y.at[y], r3y.at[y], 10, at_y(d), r3y.at[pl.ds(0, Y - 1)])

    take(11)
    s = summed(r3z, Z, 0.0)
    w4y[y, 0:16] = s[0:16]
    w4y[y, 16:24] = s[32:40]
    w4x[x, 0:16] = s[16:32]
    for d in FAR[Y]:
        send(w4y.at[y], w4y.at[y], 14, at_y(d), w4y.at[pl.ds(0, Y - 1)])
    take(10)
    s = summed(r3y, Y, 0.0)
    w4z[z] = s[0:16]
    w4x[x, 16:32] = s[16:32]
    for d in FAR[X]:
        send(w4x.at[x], w4x.at[x], 12, at_x(d), w4x.at[pl.ds(0, X - 1)])
    for d in FAR[Z]:
        send(w4z.at[z], w4z.at[z], 13, at_z(d), w4z.at[pl.ds(0, Z - 1)])

    for d in (4, 3, 5):
        send(
            merged.at[share(z, c)], merged.at[share(z, c)], 3, at_z(d),
            merged.at[pl.ds(0, SHARE * (Z - 1))],
        )

    take(12)
    f5y[c, y] = w4x[:, 0:16].reshape(64, 128)
    f5z[c, z] = w4x[:, 16:32].reshape(64, 128)
    for d in FAR[Y]:
        send(f5y.at[c, y], f5y.at[c, y], 15, at_y(d), f5y.at[0, pl.ds(0, Y - 1)])
        send(f5z.at[c, z], f5z.at[c, z], 17, at_z(d), f5z.at[0, pl.ds(0, Z - 1)])

    half_rows = piece(c, ROWS // 2)
    take(3)
    send(merged.at[half_rows], merged.at[half_rows], 18, sibling, merged.at[half_rows])
    lane = lax.broadcasted_iota(jnp.int32, (BLOCK_ROWS, 128), 1)

    def squares_of(core):
        found = jnp.zeros((BLOCK_ROWS, 128), F32)
        for k in range(BLOCKS // C):
            b = core * (BLOCKS // C) + k
            m = merged[piece(b, BLOCK_ROWS)]
            found = jnp.where(lane == b, jnp.sum(m * m, axis=1, keepdims=True), found)
        return found

    take(14)
    f5x[c, x, 0:128] = w4y[:, 0:16].reshape(128, 128)
    f5x[c, x, 256:264] = jnp.sum(w4y[:, 16:24], axis=0)
    take(13)
    f5x[c, x, 128:256] = w4z[...].reshape(128, 128)
    for d in FAR[X]:
        send(f5x.at[c, x], f5x.at[c, x], 16, at_x(d), f5x.at[0, pl.ds(0, X - 1)])

    squares = squares_of(c)
    take(18)
    squares = (squares + squares_of(sib)) * (1.0 / EMB)
    squares_row = jnp.transpose(squares)[0:BLOCKS]
    loads[-2].wait()
    state_row = state_ref[...]
    state_col = jnp.transpose(
        jnp.concatenate([state_row, jnp.zeros((BLOCK_ROWS - BLOCKS, 128), F32)], axis=0)
    )

    def squared(core, ref, n, rows):
        found = jnp.zeros((64, 128), F32)
        for k in range(n):
            for q in range(rows // 64):
                v = ref[core, k, 64 * q:64 * q + 64]
                found += v * v
        return found

    take(16)
    send(f5x.at[c], f5x.at[c], 19, sibling, f5x.at[0])
    take(15)
    send(f5y.at[c], f5y.at[c], 20, sibling, f5y.at[0])
    take(17)
    send(f5z.at[c], f5z.at[c], 21, sibling, f5z.at[0])
    mine = squared(c, f5y, Y, 64) + squared(c, f5z, Z, 64) + squared(c, f5x, X, 256)
    loads[-1].wait()
    take(19)
    take(20)
    take(21)
    other = squared(sib, f5y, Y, 64) + squared(sib, f5z, Z, 64) + squared(sib, f5x, X, 256)

    emb = f5x[:, :, 256:264]
    total = jnp.sum(mine + other, keepdims=True)
    total = total + jnp.sum(jnp.sum(emb, axis=(0, 1)), keepdims=True)
    clip = jnp.minimum(1.0, 1.0 / (jnp.sqrt(total) + 1e-06))

    clip_sq = clip * clip
    scale = (EMB_RATE * clip) / jnp.sqrt(state_col + clip_sq * squares)
    for b in range(BLOCKS):
        rows = pl.ds(b * BLOCK_ROWS, BLOCK_ROWS)
        new_table[rows] = table[rows] - merged[rows] * scale[:, b:b + 1]
    new_state[...] = state_row + clip_sq * squares_row
    rate = MLP_RATE * clip
    for core, (w, out) in enumerate(((w1, new_first), (w2, new_second))):
        for q in range(2):
            cols = pl.ds(128 * q, 128)
            for k in range(X):
                rows = pl.ds(128 * k, 128)
                g = f5x[core, k, 128 * q:128 * q + 128]
                out[rows, cols] = (w[rows, cols].astype(F32) - rate * g).astype(BF16)
        for q, ref in ((2, f5y), (3, f5z)):
            cols = pl.ds(128 * q, 128)
            g = ref[core].reshape(HID, 128)
            out[:, cols] = (w[:, cols].astype(F32) - rate * g).astype(BF16)
    finish()


def hand_over(*refs):
    *arrays, sem = refs
    n = len(arrays) // 2
    copies = [pltpu.make_async_copy(arrays[k], arrays[n + k], sem.at[k]) for k in range(n)]
    for copy in copies:
        copy.start()
    for copy in copies:
        copy.wait()


def on_device(
    table, row_state, lookup_grads, lookup_slots, lookup_rows, block_ids, block_counts,
    inputs, cotangent, w_first, w_second,
):
    hbm = pl.BlockSpec(memory_space=pl.ANY)
    vmem = pl.BlockSpec(memory_space=pltpu.VMEM)
    shapes = (
        jax.ShapeDtypeStruct((ROWS, EMB), F32),
        jax.ShapeDtypeStruct((BLOCKS, BLOCK_ROWS), F32),
        jax.ShapeDtypeStruct((HID, HID), BF16),
        jax.ShapeDtypeStruct((HID, HID), BF16),
    )
    results = pl.pallas_call(
        kernel,
        out_shape=tuple(pltpu.VMEM(a.shape, a.dtype) for a in shapes),
        in_specs=[hbm] * 11,
        out_specs=(vmem,) * 4,
        scratch_shapes=[
            pltpu.VMEM((ROWS, EMB), F32),
            pltpu.VMEM((BLOCKS, BLOCK_ROWS), F32),
            pltpu.VMEM((LOOKUPS, EMB), BF16),
            pltpu.VMEM((1, LOOKUPS), jnp.int32),
            pltpu.VMEM((1, LOOKUPS), jnp.int32),
            pltpu.SMEM((1, SLOTS), jnp.int32),
            pltpu.SMEM((1, 1), jnp.int32),
            pltpu.VMEM((HID, HID), BF16),
            pltpu.VMEM((HID, HID), BF16),
            pltpu.VMEM((2, SAMPLES, HID), BF16),
            pltpu.VMEM((2, SAMPLES, HID), BF16),
            pltpu.VMEM((ROWS, EMB), BF16),
            pltpu.VMEM((Z * C, SHARE, EMB), BF16),
            pltpu.VMEM((ROWS, EMB), F32),
            pltpu.VMEM((4, HID, 128), F32),
            pltpu.VMEM((4, HID, 128), F32),
            pltpu.VMEM((4, HID, 128), F32),
            pltpu.VMEM((X - 1, 2, 128, 128), F32),
            pltpu.VMEM((Y - 1, 64, 128), F32),
            pltpu.VMEM((Z - 1, 64, 128), F32),
            pltpu.VMEM((X, 32, 128), F32),
            pltpu.VMEM((Y, 16, 128), F32),
            pltpu.VMEM((Z, 16, 128), F32),
            pltpu.VMEM((X - 1, 32, 128), F32),
            pltpu.VMEM((Y - 1, 16, 128), F32),
            pltpu.VMEM((Z - 1, 16, 128), F32),
            pltpu.VMEM((Y, 32, 128), F32),
            pltpu.VMEM((Z, 40, 128), F32),
            pltpu.VMEM((X, 32, 128), F32),
            pltpu.VMEM((Y, 24, 128), F32),
            pltpu.VMEM((Z, 16, 128), F32),
            pltpu.VMEM((C, X, 264, 128), F32),
            pltpu.VMEM((C, Y, 64, 128), F32),
            pltpu.VMEM((C, Z, 64, 128), F32),
            pltpu.SemaphoreType.DMA((9 + 2 * SAMPLES // CHUNK,)),
            pltpu.SemaphoreType.DMA((26,)),
            pltpu.SemaphoreType.DMA((26,)),
        ],
        compiler_params=pltpu.CompilerParams(
            collective_id=0, has_side_effects=True, vmem_limit_bytes=60 * 2**20
        ),
        cost_estimate=pl.CostEstimate(
            flops=2_400_000_000, bytes_accessed=6 * 2**20, transcendentals=2**20
        ),
        name="step",
    )(
        table, row_state.reshape(BLOCKS, BLOCK_ROWS), lookup_grads, lookup_slots, lookup_rows,
        block_ids, block_counts, inputs, cotangent, w_first, w_second,
    )
    new_table, new_state, new_first, new_second = pl.pallas_call(
        hand_over,
        out_shape=shapes,
        in_specs=[vmem] * 4,
        out_specs=(hbm,) * 4,
        scratch_shapes=[pltpu.SemaphoreType.DMA((4,))],
        compiler_params=pltpu.CompilerParams(vmem_limit_bytes=16 * 2**20),
        name="hand_over",
    )(*results)
    return (new_table, new_state.reshape(ROWS), new_first, new_second)


def solution(mesh):
    placed = (
        P("table", None),
        P("table"),
        P("replica", "table", None),
        P("replica", "table"),
        P("replica", "table"),
        P("replica", "table"),
        P("replica", "table"),
        P(("replica", "table"), None),
        P(("replica", "table"), None),
        P(),
        P(),
    )
    return jax.shard_map(
        on_device,
        mesh=mesh,
        in_specs=placed,
        out_specs=(P("table", None), P("table"), P(), P()),
        check_vma=False,
    )
```

time: 62.3 us -> 59.7 us (0.958)
  Pallas kernels: 60.8 us -> 57.9 us
    pallas_call x2, Pallas kernels: 60.8 us -> 57.9 us  [the longest x1 56.7 us: on_device(): pl.pallas_call(kernel, out_shape=tuple((pltpu.VMEM(a.shape, a.dtype) for...]
where the time goes in v3:
time: 59.7 us; the launch traced here: 59.2 us
  Pallas kernels  57.9 us (97%)
  between operations  1.29 us (2%)
    pallas_call x1, Pallas kernels, on_device(): pl.pallas_call(kernel, out_shape=tuple((pltpu.VMEM(a.shape, a.dtype) for...  56.7 us

profile of v3, /device:TPU:1, one launch (start us, length us, event | category | flops | bytes accessed | tf_op | source)
XLA Modules:
  0.0 59.2 jit_solution(3687886058283110138)
XLA Ops:
  1.3 56.7 %step.1 = (f32[1024,128]{1,0:T(8,128)S(1)}, f32[8,128]{1,0:T(8,128)S(1)}, bf16[512,512]{1,0:T(8,128)(2,1)S(1)}, bf16[512,512]{1,0:T(8,128)(2,1)S(1)}) custom-call(f32[1024,128]{1,0:T(8,128)} %table_hbm.1, f32[8,128]{1,0:T(8,128)} %bitcast.2, bf16[1,1024,128]{2,1,0:T(8,128)(2,1)} %grads_hbm.1, s32[1,1024]{1,0:T(1,128)} %slots_hbm.1, s32[1,1024]{1,0:T(1,128)} %rows_hbm.1, ...), custom_call_target="tpu_custom_call" | custom-call | flops 2400000000 | bytes 6291456 | tf_op jit(solution)/shard_map/step/pallas_call | solution.py:347
  58.0 1.2 %hand_over.1 = (f32[1024,128]{1,0:T(8,128)}, f32[8,128]{1,0:T(8,128)}, bf16[512,512]{1,0:T(8,128)(2,1)}, bf16[512,512]{1,0:T(8,128)(2,1)}) custom-call(f32[1024,128]{1,0:T(8,128)S(1)} %get-tuple-element.12.refs_0_, f32[8,128]{1,0:T(8,128)S(1)} %get-tuple-element.13.refs_1_, bf16[512,512]{1,0:T(8,128)(2,1)S(1)} %get-tuple-element.14.refs_2_, ...), custom_call_target="tpu_custom_call" | custom-call | tf_op jit(solution)/shard_map/hand_over/pallas_call | solution.py:402

commit v4 on v3

--- a/solution.py
+++ b/solution.py
@@ -16,7 +16,7 @@
 ROWS = BLOCKS * BLOCK_ROWS
 SHARE = ROWS // (Z * C)
 CHUNK = 256
-PAIR = 22
+PAIR = 23
 FAR = {4: (2, 1, 3), 8: (4, 3, 5, 2, 6, 1, 7)}
 
 EMB_RATE = 0.05
@@ -72,6 +72,12 @@
                 take(k)
             pltpu.make_async_copy(whole, whole, send_sem.at[k]).wait()
 
+    barrier = pltpu.get_barrier_semaphore()
+    peers = [at_x(d) for d in range(1, X)] + [at_y(d) for d in range(1, Y)]
+    peers += [at_z(d) for d in range(1, Z)] + [at_z(d, sib) for d in range(Z)]
+    for dev in peers:
+        pl.semaphore_signal(barrier, inc=1, device_id=dev, device_id_type=MESH)
+
     parts = [pl.ds(k * CHUNK, CHUNK) for k in range(SAMPLES // CHUNK)]
     pairs = [
         (count_hbm, count_ref), (ids_hbm, ids_ref), (slots_hbm, slots_ref), (rows_hbm, rows_ref),
@@ -83,12 +89,6 @@
     loads = [pltpu.make_async_copy(*pair, in_sem.at[k]) for k, pair in enumerate(pairs)]
     for load in loads:
         load.start()
-
-    barrier = pltpu.get_barrier_semaphore()
-    peers = [at_x(d) for d in range(1, X)] + [at_y(d) for d in range(1, Y)]
-    peers += [at_z(d) for d in range(1, Z)] + [at_z(d, sib) for d in range(Z)]
-    for dev in peers:
-        pl.semaphore_signal(barrier, inc=1, device_id=dev, device_id_type=MESH)
 
     for load in loads[:5]:
         load.wait()
@@ -192,8 +192,7 @@
         send(t2z.at[lax.rem(z + d, Z)], r2z.at[d - 1], 8, at_z(d), r2z)
     for d in (2, 6, 1, 7):
         send(
-            merged.at[share(z, c)], merged.at[share(z, c)], 3, at_z(d),
-            merged.at[pl.ds(0, SHARE * (Z - 1))],
+            merged.at[share(z, c)], merged.at[share(z, c)], 3, at_z(d), merged.at[pl.ds(0, 4 * SHARE)]
         )
 
     take(5)
@@ -231,11 +230,15 @@
     for d in FAR[Z]:
         send(w4z.at[z], w4z.at[z], 13, at_z(d), w4z.at[pl.ds(0, Z - 1)])
 
-    for d in (4, 3, 5):
-        send(
-            merged.at[share(z, c)], merged.at[share(z, c)], 3, at_z(d),
-            merged.at[pl.ds(0, SHARE * (Z - 1))],
-        )
+    take(3)
+    up, down = share(lax.rem(z + 2, Z), c), share(lax.rem(z + 6, Z), c)
+    start = (c * Z) * SHARE
+    up_half = pl.ds(pl.multiple_of(start + lax.rem(z + 2, Z) * SHARE, 32), SHARE // 2)
+    down_half = pl.ds(
+        pl.multiple_of(start + lax.rem(z + 6, Z) * SHARE + SHARE // 2, 32), SHARE // 2
+    )
+    for rows, d in ((up_half, 6), (down_half, 2), (up, 7), (down, 1)):
+        send(merged.at[rows], merged.at[rows], 22, at_z(d), merged.at[pl.ds(0, 3 * SHARE)])
 
     take(12)
     f5y[c, y] = w4x[:, 0:16].reshape(64, 128)
@@ -245,7 +248,7 @@
         send(f5z.at[c, z], f5z.at[c, z], 17, at_z(d), f5z.at[0, pl.ds(0, Z - 1)])
 
     half_rows = piece(c, ROWS // 2)
-    take(3)
+    take(22)
     send(merged.at[half_rows], merged.at[half_rows], 18, sibling, merged.at[half_rows])
     lane = lax.broadcasted_iota(jnp.int32, (BLOCK_ROWS, 128), 1)
 
@@ -385,8 +388,8 @@
             pltpu.VMEM((C, Y, 64, 128), F32),
             pltpu.VMEM((C, Z, 64, 128), F32),
             pltpu.SemaphoreType.DMA((9 + 2 * SAMPLES // CHUNK,)),
-            pltpu.SemaphoreType.DMA((26,)),
-            pltpu.SemaphoreType.DMA((26,)),
+            pltpu.SemaphoreType.DMA((27,)),
+            pltpu.SemaphoreType.DMA((27,)),
         ],
         compiler_params=pltpu.CompilerParams(
             collective_id=0, has_side_effects=True, vmem_limit_bytes=60 * 2**20

time: 59.7 us -> 57.9 us (0.970)
  Pallas kernels: 57.9 us -> 56.5 us
    pallas_call x1, Pallas kernels: 56.7 us -> 55.3 us  [on_device(): pl.pallas_call(kernel, out_shape=tuple((pltpu.VMEM(a.shape, a.dtype) for...]
where the time goes in v4:
time: 57.9 us; the launch traced here: 57.8 us
  Pallas kernels  56.5 us (98%)
  between operations  1.29 us (2%)
    pallas_call x1, Pallas kernels, on_device(): pl.pallas_call(kernel, out_shape=tuple((pltpu.VMEM(a.shape, a.dtype) for...  55.3 us
    pallas_call x1, Pallas kernels, on_device(): pl.pallas_call(hand_over, out_shape=shapes, in_specs=[vmem] * 4, out_spec...  1.18 us

profile of v4, /device:TPU:1, one launch (start us, length us, event | category | flops | bytes accessed | tf_op | source)
XLA Modules:
  0.0 57.8 jit_solution(1160461312188738901)
XLA Ops:
  1.3 55.3 %step.1 = (f32[1024,128]{1,0:T(8,128)S(1)}, f32[8,128]{1,0:T(8,128)S(1)}, bf16[512,512]{1,0:T(8,128)(2,1)S(1)}, bf16[512,512]{1,0:T(8,128)(2,1)S(1)}) custom-call(f32[1024,128]{1,0:T(8,128)} %table_hbm.1, f32[8,128]{1,0:T(8,128)} %bitcast.2, bf16[1,1024,128]{2,1,0:T(8,128)(2,1)} %grads_hbm.1, s32[1,1024]{1,0:T(1,128)} %slots_hbm.1, s32[1,1024]{1,0:T(1,128)} %rows_hbm.1, ...), custom_call_target="tpu_custom_call" | custom-call | flops 2400000000 | bytes 6291456 | tf_op jit(solution)/shard_map/step/pallas_call | solution.py:350
  56.6 1.2 %hand_over.1 = (f32[1024,128]{1,0:T(8,128)}, f32[8,128]{1,0:T(8,128)}, bf16[512,512]{1,0:T(8,128)(2,1)}, bf16[512,512]{1,0:T(8,128)(2,1)}) custom-call(f32[1024,128]{1,0:T(8,128)S(1)} %get-tuple-element.12.refs_0_, f32[8,128]{1,0:T(8,128)S(1)} %get-tuple-element.13.refs_1_, bf16[512,512]{1,0:T(8,128)(2,1)S(1)} %get-tuple-element.14.refs_2_, ...), custom_call_target="tpu_custom_call" | custom-call | tf_op jit(solution)/shard_map/hand_over/pallas_call | solution.py:405

commit v5 on v4

--- a/solution.py
+++ b/solution.py
@@ -17,6 +17,13 @@
 SHARE = ROWS // (Z * C)
 CHUNK = 256
 PAIR = 23
+XA, XD, YB, ZB = 512, 512, 768, 256
+AT_D = XA
+AT_B = XA + XD
+AT_Z = XA + XD + YB
+PA, PD, PB, PZ = XA // X, XD // X, YB // Y, ZB // Z
+QA, QD, QB, QZ = PA // Y, PD // Z, PB // X, PZ // X
+PX = PA + PD
 FAR = {4: (2, 1, 3), 8: (4, 3, 5, 2, 6, 1, 7)}
 
 EMB_RATE = 0.05
@@ -111,17 +118,6 @@
     def share(zz, cc):
         return pl.ds(pl.multiple_of((cc * Z + zz) * SHARE, SHARE), SHARE)
 
-    pl.semaphore_wait(barrier, len(peers))
-    for d in FAR[Z] + (0,):
-        for core in (c, sib):
-            if d == 0 and core is c:
-                continue
-            send(
-                dense.at[share(lax.rem(z + d, Z), core)], emb_recv.at[rep], 0, at_z(d, core),
-                emb_recv.at[pl.ds(0, Z * C - 1)],
-            )
-    emb_recv[rep] = dense[share(z, c)]
-
     loads[5].wait()
     loads[6].wait()
     for k, rows in enumerate(parts):
@@ -145,31 +141,46 @@
     for half in (1, 0):
         g = grad(sib, half)
         for k in range(2):
-            block = 2 * half + k
-            g_sib[block] = g[:, 128 * k:128 * k + 128]
-            send(g_sib.at[block], g_recv.at[block], PAIR + block, sibling, g_recv.at[block])
+            g_sib[pl.ds(HID * (2 * half + k), HID)] = g[:, 128 * k:128 * k + 128]
+    pl.semaphore_wait(barrier, len(peers))
+    for k in (2, 3, 0, 1):
+        rows = pl.ds(HID * k, HID)
+        send(g_sib.at[rows], g_recv.at[rows], PAIR + k, sibling, g_recv.at[rows])
+
+    for d in FAR[Z] + (0,):
+        for core in (c, sib):
+            if d == 0 and core is c:
+                continue
+            send(
+                dense.at[share(lax.rem(z + d, Z), core)], emb_recv.at[rep], 0, at_z(d, core),
+                emb_recv.at[pl.ds(0, Z * C - 1)],
+            )
+    emb_recv[rep] = dense[share(z, c)]
+
     for half in (1, 0):
         g = grad(c, half)
-        g_own[2 * half] = g[:, :128]
-        g_own[2 * half + 1] = g[:, 128:]
-
-    def piece(k, rows):
-        return pl.ds(pl.multiple_of(k * rows, rows), rows)
+        for k in range(2):
+            g_own[pl.ds(HID * (2 * half + k), HID)] = g[:, 128 * k:128 * k + 128]
+
+    def piece(k, rows, start=0):
+        return pl.ds(pl.multiple_of(start + k * rows, 8), rows)
 
     take(PAIR + 2)
-    g_own[2] = g_own[2] + g_recv[2]
+    take(PAIR + 3)
+    g_own[2 * HID:] = g_own[2 * HID:] + g_recv[2 * HID:]
     for d in FAR[Y]:
-        send(g_own.at[2, piece(lax.rem(y + d, Y), 64)], r1y.at[d - 1], 5, at_y(d), r1y)
-    take(PAIR + 3)
-    g_own[3] = g_own[3] + g_recv[3]
-    for d in FAR[Z]:
-        send(g_own.at[3, piece(lax.rem(z + d, Z), 64)], r1z.at[d - 1], 6, at_z(d), r1z)
+        rows = piece(lax.rem(y + d, Y), PB, AT_B)
+        send(g_own.at[rows], r1y.at[d - 1], 5, at_y(d), r1y)
+        rows = piece(lax.rem(z + d, Z), PZ, AT_Z)
+        send(g_own.at[rows], r1z.at[d - 1], 6, at_z(d), r1z)
     take(PAIR)
     take(PAIR + 1)
-    g_own[0:2] = g_own[0:2] + g_recv[0:2]
+    g_own[:2 * HID] = g_own[:2 * HID] + g_recv[:2 * HID]
     for d in FAR[X]:
-        rows = piece(lax.rem(x + d, X), 128)
-        send(g_own.at[pl.ds(0, 2), rows], r1x.at[d - 1], 4, at_x(d), r1x)
+        rows = piece(lax.rem(x + d, X), PA)
+        send(g_own.at[rows], r1x.at[d - 1, pl.ds(0, PA)], 4, at_x(d), r1x)
+        rows = piece(lax.rem(x + d, X), PD, AT_D)
+        send(g_own.at[rows], r1x.at[d - 1, pl.ds(PA, PD)], 4, at_x(d), r1x)
 
     def summed(ref, n, first):
         for k in range(n):
@@ -181,12 +192,17 @@
     for k in range(1, Z * C):
         total += emb_recv[k].astype(F32)
     merged[share(z, c)] = total
-    r3z[z, 32:40] = jnp.sum((total * total).reshape(SHARE // 8, 8, EMB), axis=0)
+    r3z[z, QA + QB:QA + QB + 8] = jnp.sum((total * total).reshape(SHARE // 8, 8, EMB), axis=0)
 
     take(4)
-    s = summed(r1x, X - 1, g_own[0:2, piece(x, 128)])
-    t2y[...] = s[0].reshape(Y, 16, 128)
-    t2z[...] = s[1].reshape(Z, 16, 128)
+    s = g_own[piece(x, PA)]
+    for k in range(X - 1):
+        s = s + r1x[k, 0:PA]
+    t2y[...] = s.reshape(Y, QA, 128)
+    s = g_own[piece(x, PD, AT_D)]
+    for k in range(X - 1):
+        s = s + r1x[k, PA:PX]
+    t2z[...] = s.reshape(Z, QD, 128)
     for d in FAR[Y]:
         send(t2y.at[lax.rem(y + d, Y)], r2y.at[d - 1], 9, at_y(d), r2y)
         send(t2z.at[lax.rem(z + d, Z)], r2z.at[d - 1], 8, at_z(d), r2z)
@@ -196,35 +212,35 @@
         )
 
     take(5)
-    t2x[:, 0:16] = summed(r1y, Y - 1, g_own[2, piece(y, 64)]).reshape(X, 16, 128)
+    t2x[:, 0:QB] = summed(r1y, Y - 1, g_own[piece(y, PB, AT_B)]).reshape(X, QB, 128)
     take(6)
-    t2x[:, 16:32] = summed(r1z, Z - 1, g_own[3, piece(z, 64)]).reshape(X, 16, 128)
+    t2x[:, QB:QB + QZ] = summed(r1z, Z - 1, g_own[piece(z, PZ, AT_Z)]).reshape(X, QZ, 128)
     for d in FAR[X]:
         send(t2x.at[lax.rem(x + d, X)], r2x.at[d - 1], 7, at_x(d), r2x)
 
     take(9)
-    r3z[z, 0:16] = summed(r2y, Y - 1, t2y[y])
+    r3z[z, 0:QA] = summed(r2y, Y - 1, t2y[y])
     take(8)
-    r3y[y, 0:16] = summed(r2z, Z - 1, t2z[z])
+    r3y[y, 0:QD] = summed(r2z, Z - 1, t2z[z])
     take(7)
     s = summed(r2x, X - 1, t2x[x])
-    r3z[z, 16:32] = s[0:16]
-    r3y[y, 16:32] = s[16:32]
+    r3z[z, QA:QA + QB] = s[0:QB]
+    r3y[y, QD:QD + QZ] = s[QB:QB + QZ]
     for d in FAR[Y]:
         send(r3z.at[z], r3z.at[z], 11, at_z(d), r3z.at[pl.ds(0, Z - 1)])
         send(r3y.at[y], r3y.at[y], 10, at_y(d), r3y.at[pl.ds(0, Y - 1)])
 
     take(11)
     s = summed(r3z, Z, 0.0)
-    w4y[y, 0:16] = s[0:16]
-    w4y[y, 16:24] = s[32:40]
-    w4x[x, 0:16] = s[16:32]
+    w4y[y, 0:QA] = s[0:QA]
+    w4y[y, QA:QA + 8] = s[QA + QB:QA + QB + 8]
+    w4x[x, 0:QB] = s[QA:QA + QB]
     for d in FAR[Y]:
         send(w4y.at[y], w4y.at[y], 14, at_y(d), w4y.at[pl.ds(0, Y - 1)])
     take(10)
     s = summed(r3y, Y, 0.0)
-    w4z[z] = s[0:16]
-    w4x[x, 16:32] = s[16:32]
+    w4z[z] = s[0:QD]
+    w4x[x, QB:QB + QZ] = s[QD:QD + QZ]
     for d in FAR[X]:
         send(w4x.at[x], w4x.at[x], 12, at_x(d), w4x.at[pl.ds(0, X - 1)])
     for d in FAR[Z]:
@@ -241,8 +257,8 @@
         send(merged.at[rows], merged.at[rows], 22, at_z(d), merged.at[pl.ds(0, 3 * SHARE)])
 
     take(12)
-    f5y[c, y] = w4x[:, 0:16].reshape(64, 128)
-    f5z[c, z] = w4x[:, 16:32].reshape(64, 128)
+    f5y[c, y] = w4x[:, 0:QB].reshape(PB, 128)
+    f5z[c, z] = w4x[:, QB:QB + QZ].reshape(PZ, 128)
     for d in FAR[Y]:
         send(f5y.at[c, y], f5y.at[c, y], 15, at_y(d), f5y.at[0, pl.ds(0, Y - 1)])
         send(f5z.at[c, z], f5z.at[c, z], 17, at_z(d), f5z.at[0, pl.ds(0, Z - 1)])
@@ -261,10 +277,10 @@
         return found
 
     take(14)
-    f5x[c, x, 0:128] = w4y[:, 0:16].reshape(128, 128)
-    f5x[c, x, 256:264] = jnp.sum(w4y[:, 16:24], axis=0)
+    f5x[c, x, 0:PA] = w4y[:, 0:QA].reshape(PA, 128)
+    f5x[c, x, PX:PX + 8] = jnp.sum(w4y[:, QA:QA + 8], axis=0)
     take(13)
-    f5x[c, x, 128:256] = w4z[...].reshape(128, 128)
+    f5x[c, x, PA:PX] = w4z[...].reshape(PD, 128)
     for d in FAR[X]:
         send(f5x.at[c, x], f5x.at[c, x], 16, at_x(d), f5x.at[0, pl.ds(0, X - 1)])
 
@@ -278,12 +294,13 @@
         jnp.concatenate([state_row, jnp.zeros((BLOCK_ROWS - BLOCKS, 128), F32)], axis=0)
     )
 
-    def squared(core, ref, n, rows):
-        found = jnp.zeros((64, 128), F32)
-        for k in range(n):
-            for q in range(rows // 64):
-                v = ref[core, k, 64 * q:64 * q + 64]
-                found += v * v
+    def squared(core):
+        found = jnp.zeros((32, 128), F32)
+        for ref, n, rows in ((f5x, X, PX), (f5y, Y, PB), (f5z, Z, PZ)):
+            for k in range(n):
+                for q in range(rows // 32):
+                    v = ref[core, k, 32 * q:32 * q + 32]
+                    found += v * v
         return found
 
     take(16)
@@ -292,14 +309,14 @@
     send(f5y.at[c], f5y.at[c], 20, sibling, f5y.at[0])
     take(17)
     send(f5z.at[c], f5z.at[c], 21, sibling, f5z.at[0])
-    mine = squared(c, f5y, Y, 64) + squared(c, f5z, Z, 64) + squared(c, f5x, X, 256)
+    mine = squared(c)
     loads[-1].wait()
     take(19)
     take(20)
     take(21)
-    other = squared(sib, f5y, Y, 64) + squared(sib, f5z, Z, 64) + squared(sib, f5x, X, 256)
-
-    emb = f5x[:, :, 256:264]
+    other = squared(sib)
+
+    emb = f5x[:, :, PX:PX + 8]
     total = jnp.sum(mine + other, keepdims=True)
     total = total + jnp.sum(jnp.sum(emb, axis=(0, 1)), keepdims=True)
     clip = jnp.minimum(1.0, 1.0 / (jnp.sqrt(total) + 1e-06))
@@ -311,17 +328,17 @@
         new_table[rows] = table[rows] - merged[rows] * scale[:, b:b + 1]
     new_state[...] = state_row + clip_sq * squares_row
     rate = MLP_RATE * clip
+    spans = [(f5x, k, 0, PA * k, PA) for k in range(X)]
+    spans += [(f5x, k, PA, AT_D + PD * k, PD) for k in range(X)]
+    spans += [(f5y, k, 0, AT_B + PB * k, PB) for k in range(Y)]
+    spans += [(f5z, k, 0, AT_Z + PZ * k, PZ) for k in range(Z)]
     for core, (w, out) in enumerate(((w1, new_first), (w2, new_second))):
-        for q in range(2):
-            cols = pl.ds(128 * q, 128)
-            for k in range(X):
-                rows = pl.ds(128 * k, 128)
-                g = f5x[core, k, 128 * q:128 * q + 128]
+        for ref, k, start, row, count in spans:
+            for q in range(0, count, 32):
+                rows = pl.ds((row + q) % HID, 32)
+                cols = pl.ds((row + q) // HID * 128, 128)
+                g = ref[core, k, start + q:start + q + 32]
                 out[rows, cols] = (w[rows, cols].astype(F32) - rate * g).astype(BF16)
-        for q, ref in ((2, f5y), (3, f5z)):
-            cols = pl.ds(128 * q, 128)
-            g = ref[core].reshape(HID, 128)
-            out[:, cols] = (w[:, cols].astype(F32) - rate * g).astype(BF16)
     finish()
 
 
@@ -367,26 +384,26 @@
             pltpu.VMEM((ROWS, EMB), BF16),
             pltpu.VMEM((Z * C, SHARE, EMB), BF16),
             pltpu.VMEM((ROWS, EMB), F32),
-            pltpu.VMEM((4, HID, 128), F32),
-            pltpu.VMEM((4, HID, 128), F32),
-            pltpu.VMEM((4, HID, 128), F32),
-            pltpu.VMEM((X - 1, 2, 128, 128), F32),
-            pltpu.VMEM((Y - 1, 64, 128), F32),
-            pltpu.VMEM((Z - 1, 64, 128), F32),
-            pltpu.VMEM((X, 32, 128), F32),
-            pltpu.VMEM((Y, 16, 128), F32),
-            pltpu.VMEM((Z, 16, 128), F32),
-            pltpu.VMEM((X - 1, 32, 128), F32),
-            pltpu.VMEM((Y - 1, 16, 128), F32),
-            pltpu.VMEM((Z - 1, 16, 128), F32),
-            pltpu.VMEM((Y, 32, 128), F32),
-            pltpu.VMEM((Z, 40, 128), F32),
-            pltpu.VMEM((X, 32, 128), F32),
-            pltpu.VMEM((Y, 24, 128), F32),
-            pltpu.VMEM((Z, 16, 128), F32),
-            pltpu.VMEM((C, X, 264, 128), F32),
-            pltpu.VMEM((C, Y, 64, 128), F32),
-            pltpu.VMEM((C, Z, 64, 128), F32),
+            pltpu.VMEM((4 * HID, 128), F32),
+            pltpu.VMEM((4 * HID, 128), F32),
+            pltpu.VMEM((4 * HID, 128), F32),
+            pltpu.VMEM((X - 1, PX, 128), F32),
+            pltpu.VMEM((Y - 1, PB, 128), F32),
+            pltpu.VMEM((Z - 1, PZ, 128), F32),
+            pltpu.VMEM((X, QB + QZ, 128), F32),
+            pltpu.VMEM((Y, QA, 128), F32),
+            pltpu.VMEM((Z, QD, 128), F32),
+            pltpu.VMEM((X - 1, QB + QZ, 128), F32),
+            pltpu.VMEM((Y - 1, QA, 128), F32),
+            pltpu.VMEM((Z - 1, QD, 128), F32),
+            pltpu.VMEM((Y, QD + QZ, 128), F32),
+            pltpu.VMEM((Z, QA + QB + 8, 128), F32),
+            pltpu.VMEM((X, QB + QZ, 128), F32),
+            pltpu.VMEM((Y, QA + 8, 128), F32),
+            pltpu.VMEM((Z, QD, 128), F32),
+            pltpu.VMEM((C, X, PX + 8, 128), F32),
+            pltpu.VMEM((C, Y, PB, 128), F32),
+            pltpu.VMEM((C, Z, PZ, 128), F32),
             pltpu.SemaphoreType.DMA((9 + 2 * SAMPLES // CHUNK,)),
             pltpu.SemaphoreType.DMA((27,)),
             pltpu.SemaphoreType.DMA((27,)),

time: 57.9 us -> 57.8 us (level)
  no operation moved by 1% of the time
where the time goes in v5:
time: 57.8 us; the launch traced here: 57.6 us
  Pallas kernels  56.3 us (97%)
  between operations  1.29 us (2%)
    pallas_call x1, Pallas kernels, on_device(): pl.pallas_call(kernel, out_shape=tuple((pltpu.VMEM(a.shape, a.dtype) for...  55.2 us
    pallas_call x1, Pallas kernels, on_device(): pl.pallas_call(hand_over, out_shape=shapes, in_specs=[vmem] * 4, out_spec...  1.18 us

profile of v5, /device:TPU:1, one launch (start us, length us, event | category | flops | bytes accessed | tf_op | source)
XLA Modules:
  0.0 57.6 jit_solution(13264887507899288768)
XLA Ops:
  1.3 55.2 %step.1 = (f32[1024,128]{1,0:T(8,128)S(1)}, f32[8,128]{1,0:T(8,128)S(1)}, bf16[512,512]{1,0:T(8,128)(2,1)S(1)}, bf16[512,512]{1,0:T(8,128)(2,1)S(1)}) custom-call(f32[1024,128]{1,0:T(8,128)} %table_hbm.1, f32[8,128]{1,0:T(8,128)} %bitcast.2, bf16[1,1024,128]{2,1,0:T(8,128)(2,1)} %grads_hbm.1, s32[1,1024]{1,0:T(1,128)} %slots_hbm.1, s32[1,1024]{1,0:T(1,128)} %rows_hbm.1, ...), custom_call_target="tpu_custom_call" | custom-call | flops 2400000000 | bytes 6291456 | tf_op jit(solution)/shard_map/step/pallas_call | solution.py:367
  56.5 1.2 %hand_over.1 = (f32[1024,128]{1,0:T(8,128)}, f32[8,128]{1,0:T(8,128)}, bf16[512,512]{1,0:T(8,128)(2,1)}, bf16[512,512]{1,0:T(8,128)(2,1)}) custom-call(f32[1024,128]{1,0:T(8,128)S(1)} %get-tuple-element.12.refs_0_, f32[8,128]{1,0:T(8,128)S(1)} %get-tuple-element.13.refs_1_, bf16[512,512]{1,0:T(8,128)(2,1)S(1)} %get-tuple-element.14.refs_2_, ...), custom_call_target="tpu_custom_call" | custom-call | tf_op jit(solution)/shard_map/hand_over/pallas_call | solution.py:422
